TPU v7x, 256 devices: a whole 4x4x8 slice. The times are simulated.
256 devices in a mesh: dp: 8 (over x, core), expert: 32 (over y, z).
Axes of the slice: x: 4, y: 4, z: 8, core: 2. Of those that a mesh axis runs over, the one named last changes fastest.
Arguments:
- dense_weights: bfloat16 [3, 5632, 2048], P(None, 'dp', 'expert'), may hold values from -0.125 to 0.125
- tokens: bfloat16 [4096, 2048], P('expert'), may hold values from -6 to 6
- cotangent: bfloat16 [4096, 2048], P('expert'), may hold values from -6 to 6
- routes: int32 [4096, 4], P('expert'), may hold values from 0 to 31, all different within a row; in each aligned block of 128 rows (0 to 127, 128 to 255, ...) at most 20 rows name the same one
- route_gates: float32 [4096, 4], P('expert'), may hold values from 0.2 to 1
- unit_perm: int32 [8, 5632], replicated, may hold values from 0 to 5631, as said below
- slab_owner: int32 [32], replicated, may hold values from 0 to 31, each once
Outputs:
- mixed: bfloat16 [4096, 2048], P('expert', 'dp')
- token_grad: bfloat16 [4096, 2048], P('expert', 'dp')
- expert_grad: bfloat16 [32, 3, 1408, 2048], P('expert', None, 'dp')
Inputs may be any that keep to these rules, and one draw needn't show every extreme that they name: `unit_perm`: each row is a permutation of the 5632 units. In every row, for every slab s and share g, the 176 positions s * 1408 + g * 176 up to s * 1408 + (g + 1) * 176 - 1 hold exactly 22 units of each block of 704 consecutive units. `slab_owner`: each slab number c * 4 + s is owned by exactly one expert. `routes`: each row names 4 different experts. In each aligned block of 128 rows no expert is named more than 20 times, a bound that some block reaches.
All inputs are finite; a program needn't handle non-finite values.
Results may differ from a plain program's by a relative error of at most 0.013.
Values may be sent and summed in bfloat16 or wider, within the bound.
No kernel may reach another device: no remote copies, remote signals or barrier semaphores. Data moves between devices by JAX's collectives and lax.ppermute only.
A program may use at most 128 MiB of HBM per device.

v0:
```python
import jax
import jax.numpy as jnp
from jax import lax
from jax.sharding import PartitionSpec as P

FF = 5632
EH = 1408


def silu_parts(preact):
    sigmoid_value = jax.nn.sigmoid(preact)
    return (preact * sigmoid_value, sigmoid_value * (1.0 + preact * (1.0 - sigmoid_value)))


def contract_last(left_side, right_side):
    return lax.dot_general(
        left_side, right_side, (((1,), (1,)), ((), ())), preferred_element_type=jnp.float32
    )


def contract_first(left_side, right_side):
    return lax.dot_general(
        left_side, right_side, (((0,), (0,)), ((), ())), preferred_element_type=jnp.float32
    )


def body(dense_weights, tokens, cotangent, routes, route_gates, unit_perm, slab_owner):
    dp_count = lax.axis_size("dp")
    expert_count = lax.axis_size("expert")
    my_row = lax.axis_index("dp")
    my_col = lax.axis_index("expert")
    block_weights = lax.all_gather(dense_weights, "expert", axis=2, tiled=True)
    block_units = block_weights.shape[1]
    units_share = EH // dp_count
    pick_count = units_share // dp_count
    slab_count = FF // EH
    owned_slab = slab_owner[my_col]
    copy_id = owned_slab // slab_count
    slab_start = owned_slab % slab_count * EH
    shares = lax.dynamic_slice(unit_perm, (copy_id, slab_start), (1, EH)).reshape(
        dp_count, units_share
    )
    sort_order = jnp.argsort(shares // block_units, axis=1, stable=True)
    ordered = jnp.take_along_axis(shares, sort_order, axis=1).reshape(
        dp_count, dp_count, pick_count
    )
    my_units = lax.dynamic_index_in_dim(ordered, my_row, 1, keepdims=False) - my_row * block_units
    outgoing = jnp.take(block_weights, my_units.reshape(-1), axis=1)
    arrived = lax.all_to_all(outgoing, "dp", split_axis=1, concat_axis=1, tiled=True)
    my_order = lax.dynamic_index_in_dim(sort_order, my_row, 0, keepdims=False)
    expert_weights = jnp.take(arrived, jnp.argsort(my_order), axis=1)
    tok_rows = tokens.shape[0]
    route_count = routes.shape[1]
    copies = tok_rows * route_count
    capacity = copies * 5 // (4 * expert_count)
    flat_routes = routes.reshape(-1)
    onehot = (flat_routes[:, None] == jnp.arange(expert_count, dtype=jnp.int32)[None, :]).astype(
        jnp.int32
    )
    slot_rank = jnp.sum((jnp.cumsum(onehot, axis=0) - 1) * onehot, axis=1)
    slot_index = flat_routes * capacity + slot_rank
    source = (
        jnp.full((expert_count * capacity,), copies, jnp.int32)
        .at[slot_index]
        .set(jnp.arange(copies, dtype=jnp.int32))
    )
    filled = source < copies
    safe_rows = jnp.minimum(source, copies - 1)
    token_of = safe_rows // route_count
    pick_rows = jnp.where(filled, token_of, tok_rows)
    padded_tokens = jnp.concatenate([tokens, jnp.zeros((1, tokens.shape[1]), jnp.bfloat16)], axis=0)
    gate_of = jnp.where(filled, route_gates.reshape(-1)[safe_rows], jnp.zeros((), jnp.float32))
    send_x = padded_tokens[pick_rows]
    send_dy = (gate_of[:, None] * cotangent[token_of].astype(jnp.float32)).astype(jnp.bfloat16)
    recv_x, recv_dy = (
        lax.all_to_all(send_x, "expert", split_axis=0, concat_axis=0, tiled=True),
        lax.all_to_all(send_dy, "expert", split_axis=0, concat_axis=0, tiled=True),
    )
    w_gate = expert_weights[0]
    w_up = expert_weights[1]
    w_down = expert_weights[2]
    pre_gate = contract_last(recv_x, w_gate)
    pre_up = contract_last(recv_x, w_up)
    activation, silu_slope = silu_parts(pre_gate)
    hidden = (activation * pre_up).astype(jnp.bfloat16)
    out_part = jnp.dot(hidden, w_down, preferred_element_type=jnp.float32).astype(jnp.bfloat16)
    d_hidden = contract_last(recv_dy, w_down)
    d_gate = (d_hidden * pre_up * silu_slope).astype(jnp.bfloat16)
    d_up = (d_hidden * activation).astype(jnp.bfloat16)
    both_grads = jnp.concatenate([d_gate, d_up], axis=1)
    both_rows = jnp.concatenate([w_gate, w_up], axis=0)
    back_part = jnp.dot(both_grads, both_rows, preferred_element_type=jnp.float32).astype(
        jnp.bfloat16
    )
    weight_grads = jnp.stack(
        [
            contract_first(d_gate, recv_x),
            contract_first(d_up, recv_x),
            contract_first(hidden, recv_dy),
        ]
    ).astype(jnp.bfloat16)[None]
    shared_gate_w = block_weights[0]
    shared_up_w = block_weights[1]
    shared_down_w = block_weights[2]
    shared_gate = contract_last(tokens, shared_gate_w)
    shared_up = contract_last(tokens, shared_up_w)
    shared_act, shared_slope = silu_parts(shared_gate)
    shared_hidden = (shared_act * shared_up).astype(jnp.bfloat16)
    shared_out = jnp.dot(shared_hidden, shared_down_w, preferred_element_type=jnp.float32)
    shared_dh = contract_last(cotangent, shared_down_w)
    shared_dgate = (shared_dh * shared_up * shared_slope).astype(jnp.bfloat16)
    shared_dup = (shared_dh * shared_act).astype(jnp.bfloat16)
    shared_back = jnp.dot(
        shared_dgate, shared_gate_w, preferred_element_type=jnp.float32
    ) + jnp.dot(shared_dup, shared_up_w, preferred_element_type=jnp.float32)
    ret_out, ret_back = (
        lax.all_to_all(out_part, "expert", split_axis=0, concat_axis=0, tiled=True),
        lax.all_to_all(back_part, "expert", split_axis=0, concat_axis=0, tiled=True),
    )
    rows_out = ret_out[slot_index].astype(jnp.float32).reshape(tok_rows, route_count, -1)
    rows_back = ret_back[slot_index].astype(jnp.float32).reshape(tok_rows, route_count, -1)
    total_out = shared_out + jnp.sum(route_gates[:, :, None] * rows_out, axis=1)
    total_back = shared_back + jnp.sum(rows_back, axis=1)
    mixed, token_grad = (
        lax.psum_scatter(
            total_out.astype(jnp.bfloat16), "dp", scatter_dimension=1, tiled=True
        ).astype(jnp.float32),
        lax.psum_scatter(
            total_back.astype(jnp.bfloat16), "dp", scatter_dimension=1, tiled=True
        ).astype(jnp.float32),
    )
    return (mixed.astype(jnp.bfloat16), token_grad.astype(jnp.bfloat16), weight_grads)


def solution(mesh):
    in_specs = (
        P(None, "dp", "expert"),
        P("expert", None),
        P("expert", None),
        P("expert", None),
        P("expert", None),
        P(),
        P(),
    )
    out_specs = (P("expert", "dp"), P("expert", "dp"), P("expert", None, "dp", None))
    return jax.shard_map(body, mesh=mesh, in_specs=in_specs, out_specs=out_specs, check_vma=False)
```

profile of v0, /device:TPU:8, one launch (start us, length us, event | category | flops | bytes accessed | tf_op | source)
XLA Modules:
  0.0 516.1 jit_solution(18164291497605835355)
XLA Ops:
  7.2 0.7 all-gather.2.cloned.1.call-update
  7.9 0.8 copy.38
  8.9 1.2 reduce-window.6
  10.4 0.7 broadcast_multiply_fusion
  11.3 0.8 copy.36
  12.3 2.4 scatter_custom_fusion
  14.8 4.3 gather_fusion.4
  19.2 4.1 gather_fusion
  23.3 5.2 %all_to_all.33 = bf16[32,20,2048]{2,1,0:T(8,128)(2,1)} reshape(bf16[640,2048]{1,0:T(8,128)(2,1)} %gather_fusion) | data formatting | bytes 5242880 | tf_op jit(solution)/shard_map/all_to_all | solution.py:76
  28.5 11.8 %all-to-all-start = ((bf16[32,20,2048]{2,1,0:T(8,128)(2,1)}), bf16[32,20,2048]{2,1,0:T(8,128)(2,1)}, u32[]{:S(2)}, u32[]{:S(2)}) async-start(bf16[32,20,2048]{2,1,0:T(8,128)(2,1)} %all_to_all.33), calls=%async_computation | async-start | bytes 6291456 | tf_op jit(solution)/shard_map/all_to_all | solution.py:76
  40.4 3.4 gather_fusion.5
  43.9 3.1 reshape.189
  47.0 4.9 multiply_convert_fusion
  51.9 85.9 %all-to-all-done = bf16[32,20,2048]{2,1,0:T(8,128)(2,1)} async-done(((bf16[32,20,2048]{2,1,0:T(8,128)(2,1)}), bf16[32,20,2048]{2,1,0:T(8,128)(2,1)}, u32[]{:S(2)}, u32[]{:S(2)}) %all-to-all-start) | async-done | bytes 2621472 | tf_op jit(solution)/shard_map/all_to_all | solution.py:76
  137.8 7.4 %all-to-all-start.3 = ((bf16[32,20,2048]{2,1,0:T(8,128)(2,1)}), bf16[32,20,2048]{2,1,0:T(8,128)(2,1)}, u32[]{:S(2)}, u32[]{:S(2)}) async-start(bf16[32,20,2048]{2,1,0:T(8,128)(2,1)} %multiply_convert_fusion), calls=%async_computation.4 | async-start | bytes 6291456 | tf_op jit(solution)/shard_map/all_to_all | solution.py:77
  148.4 0.9 dynamic-slice_reduce_fusion
  149.4 3.3 sort.34
  152.8 8.6 %gather_fusion.7 = s32[1408]{0:T(1024)S(1)} fusion(s32[8,176]{1,0:T(8,128)S(1)} %reshape.185, s32[1408]{0:T(1024)S(1)} %reshape.247), kind=kCustom, calls=%fused_computation.7 | custom fusion | bytes 22528 | tf_op jit(solution)/shard_map/jit(take_along_axis)/gather | solution.py:44
  162.1 0.7 fusion.42
  163.0 27.6 %all-gather.2.cloned.1.call-done = bf16[3,704,2048]{1,2,0:T(8,128)(2,1)} async-done(((bf16[3,704,64]{1,2,0:T(8,128)(2,1)}), bf16[3,704,2048]{1,2,0:T(8,128)(2,1)}) %all-gather.2.cloned.1.call-update) | async-done | bytes 8650768 | tf_op jit(solution)/shard_map/all_gather | solution.py:32
  190.6 20.8 %copy.41 = bf16[3,704,2048]{2,0,1:T(4,128)(2,1)} copy(bf16[3,704,2048]{1,2,0:T(8,128)(2,1)} %all-gather.2.cloned.1.call-done) | data formatting | bytes 17301504 | tf_op jit(solution)/shard_map/all_gather | solution.py:32
  211.4 14.0 %gather_fusion.1 = bf16[176,3,2048]{2,1,0:T(4,128)(2,1)S(1)} fusion(bf16[3,704,2048]{2,0,1:T(4,128)(2,1)} %copy.41, s32[1024]{0:T(1024)S(1)} %pad_clamp_fusion.4), kind=kCustom, calls=%fused_computation.1 | custom fusion | bytes 4326080 | tf_op jit(solution)/shard_map/jit(_take)/gather | solution.py:48
  225.4 3.0 select_bitcast_fusion.1
  228.4 4.4 all-to-all-start.1
  232.8 3.2 sort.35
  236.0 5.2 %all_to_all.35 = bf16[640,2048]{1,0:T(8,128)(2,1)} reshape(bf16[32,20,2048]{2,1,0:T(8,128)(2,1)} %all-to-all-done) | data formatting | bytes 5242880 | tf_op jit(solution)/shard_map/all_to_all | solution.py:76
  241.2 5.2 %all_to_all.41 = bf16[640,2048]{1,0:T(8,128)(2,1)} reshape(bf16[32,20,2048]{2,1,0:T(8,128)(2,1)} %all-to-all-done.3) | data formatting | bytes 5242880 | tf_op jit(solution)/shard_map/all_to_all | solution.py:77
  246.4 22.0 %all-to-all-done.1 = bf16[3,176,2048]{2,0,1:T(4,128)(2,1)S(1)} async-done(((bf16[3,176,2048]{2,0,1:T(4,128)(2,1)}), bf16[3,176,2048]{2,0,1:T(4,128)(2,1)S(1)}, u32[]{:S(2)}, u32[]{:S(2)}) %all-to-all-start.1) | async-done | bytes 2162720 | tf_op jit(solution)/shard_map/all_to_all | solution.py:49
  268.4 9.5 %gather_fusion.2 = bf16[176,3,2048]{2,1,0:T(4,128)(2,1)} fusion(bf16[3,176,2048]{2,0,1:T(4,128)(2,1)S(1)} %all-to-all-done.1, s32[1024]{0:T(1024)S(1)} %pad_clamp_fusion.3), kind=kCustom, calls=%fused_computation.2 | custom fusion | bytes 4326080 | tf_op jit(solution)/shard_map/jit(_take)/gather | solution.py:51
  277.9 3.2 select_bitcast_fusion
  281.1 3.1 fusion.43
  285.1 1.4 copy-done.2
  286.5 1.0 fusion.44
  287.6 0.7 copy-done.4
  288.3 1.2 fusion.17
  289.5 1.2 multiply_convert_fusion.2
  291.4 1.6 convolution_convert_fusion.1
  293.0 2.4 all_to_all.42
  295.4 9.1 %all-to-all-start.4 = ((bf16[32,20,2048]{2,1,0:T(8,128)(2,1)}), bf16[32,20,2048]{2,1,0:T(8,128)(2,1)}, u32[]{:S(2)}, u32[]{:S(2)}) async-start(bf16[32,20,2048]{2,1,0:T(8,128)(2,1)} %all_to_all.42), calls=%async_computation.5 | async-start | bytes 6291456 | tf_op jit(solution)/shard_map/all_to_all | solution.py:118
  304.5 2.3 convolution_convert_fusion
  306.8 2.4 all_to_all.37
  309.2 67.3 %all-to-all-done.4 = bf16[32,20,2048]{2,1,0:T(8,128)(2,1)} async-done(((bf16[32,20,2048]{2,1,0:T(8,128)(2,1)}), bf16[32,20,2048]{2,1,0:T(8,128)(2,1)}, u32[]{:S(2)}, u32[]{:S(2)}) %all-to-all-start.4) | async-done | bytes 2621472 | tf_op jit(solution)/shard_map/all_to_all | solution.py:118
  376.5 8.4 %all-to-all-start.2 = ((bf16[32,20,2048]{2,1,0:T(8,128)(2,1)}), bf16[32,20,2048]{2,1,0:T(8,128)(2,1)}, u32[]{:S(2)}, u32[]{:S(2)}) async-start(bf16[32,20,2048]{2,1,0:T(8,128)(2,1)} %all_to_all.37), calls=%async_computation.2 | async-start | bytes 6291456 | tf_op jit(solution)/shard_map/all_to_all | solution.py:117
  385.0 3.2 fusion.1
  388.2 3.3 fusion.3
  391.5 3.3 fusion.4
  394.9 0.7 copy-done.12
  395.6 4.1 fusion
  399.7 3.6 all_to_all.44
  403.3 3.3 gather_fusion.6
  406.6 4.8 reshape.190
  411.3 4.9 reduce_sum.32
  416.3 4.0 fusion.10
  420.7 36.0 %all-to-all-done.2 = bf16[32,20,2048]{2,1,0:T(8,128)(2,1)} async-done(((bf16[32,20,2048]{2,1,0:T(8,128)(2,1)}), bf16[32,20,2048]{2,1,0:T(8,128)(2,1)}, u32[]{:S(2)}, u32[]{:S(2)}) %all-to-all-start.2) | async-done | bytes 2621472 | tf_op jit(solution)/shard_map/all_to_all | solution.py:117
  456.7 3.6 all_to_all.39
  460.3 3.3 gather_fusion.3
  463.6 4.8 reshape.188
  468.4 5.5 %multiply_reduce_fusion = f32[128,2048]{1,0:T(8,128)S(1)} fusion(f32[128,4,2048]{2,1,0:T(4,128)} %reshape.188, f32[128,4]{1,0:T(8,128)S(1)} %copy.36), kind=kLoop, calls=%fused_computation.10 | loop fusion | flops 1835008 | bytes 5244928 | tf_op jit(solution)/shard_map/reduce_sum | solution.py:122
  473.9 3.9 fusion.9
  477.8 2.6 fusion.13
  480.5 0.8 fusion.11
  481.4 0.7 fusion.12
  482.1 1.6 pad_maximum_fusion
  483.7 25.4 %reduce-scatter.3.cloned.1.call-done = bf16[128,256]{1,0:T(8,128)(2,1)} async-done(((bf16[128,2048]{1,0:T(8,128)(2,1)}), bf16[128,256]{1,0:T(8,128)(2,1)}) %reduce-scatter.3.cloned.1.call-update) | async-done | bytes 65552 | tf_op jit(solution)/shard_map/reduce_scatter | solution.py:125
  (84 shorter events, 5.0 us)
Async XLA Ops:
  7.2 33.3 %copy-start = (bf16[128,2048]{1,0:T(8,128)(2,1)S(1)}, bf16[128,2048]{1,0:T(8,128)(2,1)}, u32[]{:S(2)}) copy-start(bf16[128,2048]{1,0:T(8,128)(2,1)} %param.9) | copy-start | bytes 1572868
  7.2 11.9 %copy-start.5 = (bf16[128,2048]{1,0:T(8,128)(2,1)S(1)}, bf16[128,2048]{1,0:T(8,128)(2,1)}, u32[]{:S(2)}) copy-start(bf16[128,2048]{1,0:T(8,128)(2,1)} %param.8) | copy-start | bytes 1572868
  7.2 183.4 %all-gather.2.cloned.1.call-start = ((), (), s32[]{:S(2)}) async-start(), calls=%async_computation.7 | async-start | bytes 9732096 | tf_op jit(solution)/shard_map/all_gather | solution.py:32
  28.5 109.3 %all-to-all-start = ((bf16[32,20,2048]{2,1,0:T(8,128)(2,1)}), bf16[32,20,2048]{2,1,0:T(8,128)(2,1)}, u32[]{:S(2)}, u32[]{:S(2)}) async-start(bf16[32,20,2048]{2,1,0:T(8,128)(2,1)} %all_to_all.33), calls=%async_computation | async-start | bytes 6291456 | tf_op jit(solution)/shard_map/all_to_all | solution.py:76
  51.9 93.3 %copy-start.7 = (s32[32]{0:T(128)S(1)}, s32[32]{0:T(128)}, u32[]{:S(2)}) copy-start(s32[32]{0:T(128)} %param.13) | copy-start | bytes 388
  137.8 90.6 %all-to-all-start.3 = ((bf16[32,20,2048]{2,1,0:T(8,128)(2,1)}), bf16[32,20,2048]{2,1,0:T(8,128)(2,1)}, u32[]{:S(2)}, u32[]{:S(2)}) async-start(bf16[32,20,2048]{2,1,0:T(8,128)(2,1)} %multiply_convert_fusion), calls=%async_computation.4 | async-start | bytes 6291456 | tf_op jit(solution)/shard_map/all_to_all | solution.py:77
  228.4 40.0 %all-to-all-start.1 = ((bf16[3,176,2048]{2,0,1:T(4,128)(2,1)}), bf16[3,176,2048]{2,0,1:T(4,128)(2,1)S(1)}, u32[]{:S(2)}, u32[]{:S(2)}) async-start(bf16[3,176,2048]{2,0,1:T(4,128)(2,1)} %select_bitcast_fusion.1), calls=%async_computation.1 | async-start | bytes 5767168 | tf_op jit(solution)/shard_map/all_to_all | solution.py:49
  284.3 3.3 copy-start.1
  284.3 2.3 copy-start.2
  286.5 1.7 copy-start.4
  290.6 0.7 copy-start.13
  290.6 0.8 copy-start.15
  295.4 81.1 %all-to-all-start.4 = ((bf16[32,20,2048]{2,1,0:T(8,128)(2,1)}), bf16[32,20,2048]{2,1,0:T(8,128)(2,1)}, u32[]{:S(2)}, u32[]{:S(2)}) async-start(bf16[32,20,2048]{2,1,0:T(8,128)(2,1)} %all_to_all.42), calls=%async_computation.5 | async-start | bytes 6291456 | tf_op jit(solution)/shard_map/all_to_all | solution.py:118
  309.2 75.8 %copy-start.6 = (bf16[128,2048]{1,0:T(8,128)(2,1)S(1)}, bf16[128,2048]{1,0:T(8,128)(2,1)}, u32[]{:S(2)}) copy-start(bf16[128,2048]{1,0:T(8,128)(2,1)} %param.8) | copy-start | bytes 1572868
  376.5 80.2 %all-to-all-start.2 = ((bf16[32,20,2048]{2,1,0:T(8,128)(2,1)}), bf16[32,20,2048]{2,1,0:T(8,128)(2,1)}, u32[]{:S(2)}, u32[]{:S(2)}) async-start(bf16[32,20,2048]{2,1,0:T(8,128)(2,1)} %all_to_all.37), calls=%async_computation.2 | async-start | bytes 6291456 | tf_op jit(solution)/shard_map/all_to_all | solution.py:117
  384.9 98.8 %reduce-scatter.5.cloned.1.call-start = ((), (), s32[]{:S(2)}) async-start(), calls=%async_computation.9 | async-start | bytes 589824 | tf_op jit(solution)/shard_map/reduce_scatter | solution.py:128
  388.2 6.7 %copy-start.9 = (f32[128,704]{0,1:T(8,128)}, f32[128,704]{0,1:T(8,128)S(1)}, u32[]{:S(2)}) copy-start(f32[128,704]{0,1:T(8,128)S(1)} %fusion.1) | copy-start | bytes 1081348
  391.5 3.3 copy-start.17
  394.9 0.7 copy-start.12
  411.3 5.0 copy-start.8
  411.3 5.0 copy-start.10
  420.4 88.7 %reduce-scatter.3.cloned.1.call-start = ((), (), s32[]{:S(2)}) async-start(), calls=%async_computation.8 | async-start | bytes 589824 | tf_op jit(solution)/shard_map/reduce_scatter | solution.py:125
  468.4 5.5 %copy-start.11 = (f32[128,704]{0,1:T(8,128)S(1)}, f32[128,704]{0,1:T(8,128)}, u32[]{:S(2)}) copy-start(f32[128,704]{0,1:T(8,128)} %copy-done.9) | copy-start | bytes 1081348
  468.4 5.5 %copy-start.18 = (f32[128,704]{0,1:T(8,128)S(1)}, f32[128,704]{0,1:T(8,128)}, u32[]{:S(2)}) copy-start(f32[128,704]{0,1:T(8,128)} %copy-done.17) | copy-start | bytes 1081348
  477.8 2.7 copy-start.3
  477.8 2.7 copy-start.16
  480.5 0.9 copy-start.14
Sparse Core Ops, SparseCore 0:
  10.6 179.9 all-gather.1
  420.5 33.3 reduce-scatter.4
  477.9 31.1 reduce-scatter.2
where the time goes:
time: 523 us; the launch traced here: 516 us
  waiting for transfers between devices  265 us (51%)
  local copies, waits for them, and re-layouts  127 us (24%)
  starting transfers between devices  41.5 us (8%)
  matrix products  33.2 us (6%)
  other arithmetic  32.4 us (6%)
  between operations  17.4 us (3%)
    all_to_all x1, waiting for transfers between devices, body(): lax.all_to_all(send_x, 'expert', split_axis=0, concat_axis=0, tiled=True)  85.9 us
    all_to_all x1, waiting for transfers between devices, body(): lax.all_to_all(back_part, 'expert', split_axis=0, concat_axis=0, tiled=True)  67.3 us
    all_to_all x1, waiting for transfers between devices, body(): lax.all_to_all(out_part, 'expert', split_axis=0, concat_axis=0, tiled=True)  36 us
    all_gather x1, waiting for transfers between devices, body(): block_weights = lax.all_gather(dense_weights, 'expert', axis=2, tiled=True)  27.6 us
    reduce_scatter x1, waiting for transfers between devices, body(): lax.psum_scatter(total_out.astype(jnp.bfloat16), 'dp', scatter_dimension=...  25.4 us
    all_to_all x1, waiting for transfers between devices, body(): lax.all_to_all(outgoing, 'dp', split_axis=1, concat_axis=1, tiled=True)  22 us
    all_gather x1, local copies, waits for them, and re-layouts, body(): block_weights = lax.all_gather(dense_weights, 'expert', axis=2, tiled=True)  20.8 us
    gather x1, local copies, waits for them, and re-layouts, body(): outgoing = jnp.take(block_weights, my_units.reshape(-1), axis=1)  14 us
  transfers between devices with their start and end apart: 8, of which 6 were waited for; matrix products, arithmetic and copies ran while one was open for 27% of the time, Pallas kernels for 0%

commit v1 on v0

v1 whole, which is shorter than its diff:
```python
import jax
import jax.numpy as jnp
import numpy as np
from jax import lax
from jax.experimental import pallas as pl
from jax.experimental.pallas import tpu as pltpu
from jax.sharding import Mesh, PartitionSpec as P

NX, NC, NY, NZ = 4, 2, 4, 8
DP, EXPERT = ("x", "c"), ("y", "z")
SIZE = {"x": NX, "c": NC, "y": NY, "z": NZ}
D = 2048
EH = 1408
UNITS = 704
HALF = UNITS // 2
SHARE = 176
PICK = 22
PAD = 32
CAP = 20
TOK = 128
N_DP, N_EXP = 8, 32
SLOTS = N_EXP * CAP
ROWS = 2 * SLOTS
COLS = D // N_DP
PART_A = 640
PART_B = 3 * HALF - PART_A
F32, BF16 = jnp.float32, jnp.bfloat16
VMEM_LIMIT = 60 * 1024 * 1024
Z_FROM = (0, -1, 1, -2, 2, -3, 3, 4)
Y_FROM = (0, -1, 1, 2)


def shift(value, axis, by):
    size = SIZE[axis]
    return lax.ppermute(value, axis, [(i, (i + by) % size) for i in range(size)])


def dot(lhs, rhs):
    return jnp.dot(lhs, rhs, preferred_element_type=F32)


def dot_last(lhs, rhs):
    return lax.dot_general(lhs, rhs, (((1,), (1,)), ((), ())), preferred_element_type=F32)


def dot_first(lhs, rhs):
    return lax.dot_general(lhs, rhs, (((0,), (0,)), ((), ())), preferred_element_type=F32)


def split3(value):
    high = value.astype(BF16)
    rest = value - high.astype(F32)
    middle = rest.astype(BF16)
    return high, middle, (rest - middle.astype(F32)).astype(BF16)


def silu_parts(preact):
    sigmoid_value = jax.nn.sigmoid(preact)
    return preact * sigmoid_value, sigmoid_value * (1.0 + preact * (1.0 - sigmoid_value))


def vmem():
    return pl.BlockSpec(memory_space=pltpu.VMEM)


def smem():
    return pl.BlockSpec(memory_space=pltpu.SMEM)


def hbm():
    return pl.BlockSpec(memory_space=pl.ANY)


def params():
    return pltpu.CompilerParams(vmem_limit_bytes=VMEM_LIMIT)


def slot_columns():
    column = np.arange(ROWS)
    table = np.zeros((8, ROWS), np.int32)
    table[0] = column // (2 * CAP)
    table[1] = column % (2 * CAP) // CAP
    table[2] = column % CAP
    return jnp.asarray(table)


def order_matrix():
    matrix = np.zeros((160, 160), np.float32)
    for b in range(4):
        for p in range(2):
            for r in range(CAP):
                matrix[p * 80 + b * CAP + r, b * 40 + p * CAP + r] = 1
    return jnp.asarray(matrix, BF16)


def pair_matrix():
    matrix = np.zeros((256, 256), np.float32)
    for i in range(64):
        matrix[i, i] = 1
        matrix[64 + i, 128 + i] = 1
        matrix[128 + i, 64 + i] = 1
        matrix[192 + i, 192 + i] = 1
    return jnp.asarray(matrix, BF16)


def slot_masks(routes_ref, gates_ref, table_ref):
    expert = table_ref[0:1, :]
    part = table_ref[1:2, :]
    rank = table_ref[2:3, :].astype(F32)
    named = jnp.zeros((TOK, ROWS), F32)
    gate = jnp.zeros((TOK, ROWS), F32)
    for k in range(4):
        hit = routes_ref[:, k : k + 1] == expert
        named = named + jnp.where(hit, 1.0, 0.0)
        gate = gate + jnp.where(hit, gates_ref[:, k : k + 1], 0.0)
    row = lax.broadcasted_iota(jnp.int32, (TOK, TOK), 0)
    col = lax.broadcasted_iota(jnp.int32, (TOK, TOK), 1)
    before = jnp.where(col < row, 1.0, 0.0).astype(BF16)
    place = dot(before, named.astype(BF16))
    slot = jnp.where((place == rank) & (named > 0.5), 1.0, 0.0)
    first = jnp.where(part == 0, slot, 0.0)
    second = jnp.where(part == 1, slot, 0.0)
    return first, second, gate


def send_kernel(place_ref, routes_ref, gates_ref, table_ref, tokens_ref, cot_ref, out_ref):
    first, second, gate = slot_masks(routes_ref, gates_ref, table_ref)
    columns = pl.ds(pl.multiple_of(place_ref[0] * COLS, COLS), COLS)
    rows_x = dot_first(first.astype(BF16), tokens_ref[:, columns])
    rows_dy = dot_first(second.astype(BF16), cot_ref[:, columns])
    ones = jnp.ones((TOK, COLS), BF16)
    scale = jnp.zeros((ROWS, COLS), F32)
    for piece in split3(second * gate):
        scale = scale + dot_first(piece, ones)
    out_ref[...] = (rows_x + rows_dy * scale).astype(BF16)


def order_in_kernel(order_ref, in_ref, out_ref):
    for b in range(8):
        rows = dot(order_ref[...], in_ref[160 * b : 160 * (b + 1), :]).astype(BF16)
        out_ref[80 * b : 80 * (b + 1), :] = rows[:80]
        out_ref[SLOTS + 80 * b : SLOTS + 80 * (b + 1), :] = rows[80:]


def order_out_kernel(order_ref, in_ref, out_ref):
    for b in range(8):
        rows = jnp.concatenate(
            [in_ref[80 * b : 80 * (b + 1), :], in_ref[SLOTS + 80 * b : SLOTS + 80 * (b + 1), :]],
            axis=0,
        )
        out_ref[160 * b : 160 * (b + 1), :] = dot_first(order_ref[...], rows).astype(BF16)


def combine_kernel(routes_ref, gates_ref, table_ref, back_ref, sums_ref, mixed_ref, grad_ref):
    first, second, gate = slot_masks(routes_ref, gates_ref, table_ref)
    rows = back_ref[...]
    mixed = sums_ref[ROWS : ROWS + TOK, :].astype(F32)
    for piece in split3(first * gate):
        mixed = mixed + dot(piece, rows)
    mixed_ref[...] = mixed.astype(BF16)
    grad = sums_ref[ROWS + TOK : ROWS + 2 * TOK, :].astype(F32) + dot(second.astype(BF16), rows)
    grad_ref[...] = grad.astype(BF16)


def block_copies(refs, gathered, place_ref, sems):
    a_refs, b_refs = refs[:5], refs[5:]
    y, z = place_ref[1], place_ref[2]
    copies = []

    def add(source, device_y, device_z, start, count):
        e = lax.rem(device_y + 2 * NY, NY) * NZ + lax.rem(device_z + 2 * NZ, NZ)
        copies.append(
            pltpu.make_async_copy(
                source, gathered.at[e, pl.ds(start, count)], sems.at[len(copies) % 8]
            )
        )

    for i, dy in enumerate(Y_FROM):
        for j, dz in enumerate(Z_FROM):
            if i < 3:
                source = a_refs[i].at[pl.ds(j * PART_A, PART_A)]
            else:
                source = a_refs[3 + j // 4].at[pl.ds(j % 4 * PART_A, PART_A)]
            add(source, y + dy, z + dz, 0, PART_A)
    for j, dz in enumerate(Z_FROM):
        for i, dy in enumerate(Y_FROM):
            if j < 7:
                source = b_refs[j].at[pl.ds(i * PART_B, PART_B)]
            else:
                source = b_refs[7 + i // 2].at[pl.ds(i % 2 * PART_B, PART_B)]
            add(source, y + dy, z + dz, PART_A, PART_B)
    return copies


def expert_kernel(*refs):
    place_ref = refs[0]
    pieces = refs[1:15]
    rows_ref, tokens_ref, cot_ref, pick_ref, pair_ref = refs[15:20]
    big_ref, acts_ref = refs[20:22]
    gathered, weights, rows, picked, sems, row_sems = refs[22:]
    copies = block_copies(pieces, gathered, place_ref, sems)
    row_copies = [
        pltpu.make_async_copy(
            rows_ref.at[g], rows.at[:, pl.ds(g * COLS, COLS)], row_sems.at[g]
        )
        for g in range(N_DP)
    ]
    for copy in copies + row_copies:
        copy.start()
    unit = lax.broadcasted_iota(jnp.int32, (N_DP * PAD, UNITS), 1)
    pick = jnp.where(pick_ref[...] == unit, 1.0, 0.0).astype(BF16)
    for copy in copies:
        copy.wait()

    def assemble(g, carry):
        for half in range(2):
            j = 2 * g + half
            both = jnp.concatenate([gathered[2 * j], gathered[2 * j + 1]], axis=1)
            mixed = dot(both, pair_ref[...]).astype(BF16)
            lanes = pl.ds(pl.multiple_of(j * 128, 128), 128)
            for m in range(3):
                part = mixed[m * HALF : (m + 1) * HALF]
                weights[m, :HALF, lanes] = part[:, :128]
                weights[m, HALF:, lanes] = part[:, 128:]
        lanes = pl.ds(pl.multiple_of(g * COLS, COLS), COLS)
        for m in range(3):
            picked[m, :, lanes] = dot(pick, weights[m, :, lanes]).astype(BF16)
        return carry

    lax.fori_loop(0, N_DP, assemble, 0)

    shared_gate = dot_last(tokens_ref[...], weights[0])
    shared_up = dot_last(tokens_ref[...], weights[1])
    shared_dh = dot_last(cot_ref[...], weights[2])
    act, slope = silu_parts(shared_gate)
    shared_hidden = (act * shared_up).astype(BF16)
    shared_dgate = (shared_dh * shared_up * slope).astype(BF16)
    shared_dup = (shared_dh * act).astype(BF16)

    for copy in row_copies:
        copy.wait()
    gate = dot_last(picked[0], rows[:SLOTS])
    up = dot_last(picked[1], rows[:SLOTS])
    dh = dot_last(picked[2], rows[SLOTS:])
    act, slope = silu_parts(gate)
    hidden = act * up
    dgate = dh * up * slope
    dup = dh * act
    hidden_t = hidden.T.astype(BF16)
    dgate_t = dgate.T.astype(BF16)
    dup_t = dup.T.astype(BF16)
    for m, value in enumerate((dgate, dup, hidden)):
        value = value.astype(BF16)
        for s in range(N_DP):
            acts_ref[s, m * PAD : (m + 1) * PAD, :] = value[s * PAD : (s + 1) * PAD]

    def outputs(g, carry):
        lanes = pl.ds(pl.multiple_of(g * COLS, COLS), COLS)
        big_ref[g, :SLOTS, :] = dot(hidden_t, picked[2, :, lanes]).astype(BF16)
        big_ref[g, SLOTS:ROWS, :] = (
            dot(dgate_t, picked[0, :, lanes]) + dot(dup_t, picked[1, :, lanes])
        ).astype(BF16)
        big_ref[g, ROWS : ROWS + TOK, :] = dot(shared_hidden, weights[2, :, lanes]).astype(BF16)
        big_ref[g, ROWS + TOK :, :] = (
            dot(shared_dgate, weights[0, :, lanes]) + dot(shared_dup, weights[1, :, lanes])
        ).astype(BF16)
        return carry

    lax.fori_loop(0, N_DP, outputs, 0)


def grad_kernel(code_ref, acts_ref, rows_ref, out_ref):
    column = lax.broadcasted_iota(jnp.int32, (SHARE, N_DP * PAD), 1)
    order = jnp.where(code_ref[...] == column, 1.0, 0.0).astype(BF16)
    for m in range(3):
        acts = jnp.concatenate(
            [acts_ref[b, m * PAD : (m + 1) * PAD, :] for b in range(N_DP)], axis=0
        )
        mine = dot(order, acts).astype(BF16)
        start = SLOTS if m == 2 else 0
        for g in range(N_DP):
            out_ref[m, :, g * COLS : (g + 1) * COLS] = dot(
                mine, rows_ref[g, start : start + SLOTS, :]
            ).astype(BF16)


def gather_weights(dense_weights):
    packed = jnp.concatenate([dense_weights[:, :HALF], dense_weights[:, HALF:]], axis=2)
    packed = packed.reshape(3 * HALF, 128)

    def along_z(own):
        half = own.shape[0] // 2
        f1, b1 = shift(own, "z", 1), shift(own, "z", -1)
        f2, b2 = shift(own, "z", 2), shift(own, "z", -2)
        f3, b3 = shift(f2, "z", 1), shift(b2, "z", -1)
        return [own, f1, b1, f2, b2, f3, b3, shift(f2[:half], "z", 2), shift(b2[half:], "z", -2)]

    def along_y(own):
        half = own.shape[0] // 2
        f, b = shift(own, "y", 1), shift(own, "y", -1)
        return [own, f, b, shift(f[:half], "y", 1), shift(b[half:], "y", -1)]

    part_a = along_y(jnp.concatenate(along_z(packed[:PART_A])))
    part_b = along_z(jnp.concatenate(along_y(packed[PART_A:])))
    return part_a + part_b


def body(dense_weights, tokens, cotangent, routes, route_gates, unit_perm, slab_owner):
    g = lax.axis_index(DP)
    y, z = lax.axis_index("y"), lax.axis_index("z")
    place = jnp.stack([g, y, z]).astype(jnp.int32)
    pieces = gather_weights(dense_weights)

    owned = slab_owner[y * NZ + z]
    units = lax.dynamic_slice(unit_perm, (owned // 4, owned % 4 * EH), (1, EH)).reshape(N_DP, SHARE)
    block = units // UNITS
    inside = block == g
    rank = jnp.cumsum(inside.astype(jnp.int32), axis=1) - 1
    spot = jnp.arange(PAD, dtype=jnp.int32)
    taken = inside[:, None, :] & (rank[:, None, :] == spot[None, :, None])
    pick = jnp.sum(jnp.where(taken, (units - g * UNITS + 1)[:, None, :], 0), axis=2) - 1
    pick = pick.reshape(N_DP * PAD, 1)
    mine = lax.dynamic_index_in_dim(block, g, 0, keepdims=False)
    earlier = jnp.tril(jnp.ones((SHARE, SHARE), jnp.bool_), -1)
    code = mine * PAD + jnp.sum((mine[:, None] == mine[None, :]) & earlier, axis=1, dtype=jnp.int32)
    code = code.reshape(SHARE, 1)

    table, order = slot_columns(), order_matrix()
    send = pl.pallas_call(
        send_kernel,
        out_shape=jax.ShapeDtypeStruct((ROWS, COLS), BF16),
        in_specs=[smem()] + [vmem()] * 5,
        out_specs=vmem(),
        compiler_params=params(),
    )(place, routes, route_gates, table, tokens, cotangent)
    received = lax.all_to_all(
        send.reshape(N_EXP, 2 * CAP, COLS), EXPERT, split_axis=0, concat_axis=0, tiled=True
    ).reshape(ROWS, COLS)
    ordered = pl.pallas_call(
        order_in_kernel,
        out_shape=jax.ShapeDtypeStruct((ROWS, COLS), BF16),
        in_specs=[vmem()] * 2,
        out_specs=vmem(),
        compiler_params=params(),
    )(order, received)
    rows = lax.all_gather(ordered, DP, axis=0, tiled=False)

    big, acts = pl.pallas_call(
        expert_kernel,
        out_shape=(
            jax.ShapeDtypeStruct((N_DP, ROWS + 2 * TOK, COLS), BF16),
            jax.ShapeDtypeStruct((N_DP, 3 * PAD, SLOTS), BF16),
        ),
        in_specs=[smem()] + [hbm()] * 15 + [vmem()] * 4,
        out_specs=(vmem(), vmem()),
        scratch_shapes=[
            pltpu.VMEM((N_EXP, 3 * HALF, 128), BF16),
            pltpu.VMEM((3, UNITS, D), BF16),
            pltpu.VMEM((ROWS, D), BF16),
            pltpu.VMEM((3, N_DP * PAD, D), BF16),
            pltpu.SemaphoreType.DMA((8,)),
            pltpu.SemaphoreType.DMA((N_DP,)),
        ],
        compiler_params=params(),
    )(place, *pieces, rows, tokens, cotangent, pick, pair_matrix())

    sums = lax.psum_scatter(big, DP, scatter_dimension=0, tiled=False)
    sums = sums.reshape(ROWS + 2 * TOK, COLS)
    back = pl.pallas_call(
        order_out_kernel,
        out_shape=jax.ShapeDtypeStruct((ROWS, COLS), BF16),
        in_specs=[vmem()] * 2,
        out_specs=vmem(),
        compiler_params=params(),
    )(order, sums)
    back = lax.all_to_all(
        back.reshape(N_EXP, 2 * CAP, COLS), EXPERT, split_axis=0, concat_axis=0, tiled=True
    ).reshape(ROWS, COLS)
    mixed, token_grad = pl.pallas_call(
        combine_kernel,
        out_shape=(jax.ShapeDtypeStruct((TOK, COLS), BF16),) * 2,
        in_specs=[vmem()] * 5,
        out_specs=(vmem(), vmem()),
        compiler_params=params(),
    )(routes, route_gates, table, back, sums)

    acts = lax.all_to_all(acts, DP, split_axis=0, concat_axis=0, tiled=True)
    grads = pl.pallas_call(
        grad_kernel,
        out_shape=jax.ShapeDtypeStruct((3, SHARE, D), BF16),
        in_specs=[vmem()] * 3,
        out_specs=vmem(),
        compiler_params=params(),
    )(code, acts, rows)
    return mixed, token_grad, grads[None]


def solution(mesh):
    mesh = Mesh(mesh.devices.reshape(NX, NC, NY, NZ), ("x", "c", "y", "z"))
    in_specs = (
        P(None, DP, EXPERT),
        P(EXPERT, None),
        P(EXPERT, None),
        P(EXPERT, None),
        P(EXPERT, None),
        P(),
        P(),
    )
    out_specs = (P(EXPERT, DP), P(EXPERT, DP), P(EXPERT, None, DP, None))
    return jax.shard_map(body, mesh=mesh, in_specs=in_specs, out_specs=out_specs, check_vma=False)
```

time: 523 us -> 284 us (0.54)
  waiting for transfers between devices: 265 us -> 114 us
  local copies, waits for them, and re-layouts: 127 us -> 20 us
  Pallas kernels: 0 us -> 47.9 us
  matrix products: 33.2 us -> 0 us
  blocking collectives: 0 us -> 29.8 us
  other arithmetic: 32.4 us -> 3.6 us
  starting transfers between devices: 41.5 us -> 48.3 us
    all_to_all x5 -> x2, waiting for transfers between devices: 211 us -> 9.27 us  [the longest x1 9.27 us: body(): lax.all_to_all(back.reshape(N_EXP, 2 * CAP, COLS), EXPERT, split_axis=0,...]
    ppermute x0 -> x24, waiting for transfers between devices: none -> 59.3 us  [shift(): lax.ppermute(value, axis, [(i, (i + by) % size) for i in range(size)])]
    gather x10 -> x0, local copies, waits for them, and re-layouts: 50.7 us -> none  [the longest x1 14 us: body(): outgoing = jnp.take(block_weights, my_units.reshape(-1), axis=1)]
    pallas_call x0 -> x6, Pallas kernels: none -> 47.9 us  [the longest x1 29.5 us: body(): pl.pallas_call(expert_kernel, out_shape=(jax.ShapeDtypeStruct((N_DP, ROWS...]
    ppermute x0 -> x24, starting transfers between devices: none -> 36 us  [shift(): lax.ppermute(value, axis, [(i, (i + by) % size) for i in range(size)])]
    dot_general x14 -> x0, matrix products: 33.2 us -> none  [the longest x6 13.2 us: contract_last(): lax.dot_general(left_side, right_side, (((1,), (1,)), ((), ())), preferre...]
    all_to_all x0 -> x1, blocking collectives: none -> 29.8 us  [body(): lax.all_to_all(send.reshape(N_EXP, 2 * CAP, COLS), EXPERT, split_axis=0,...]
    all_to_all x5 -> x2, starting transfers between devices: 41.1 us -> 12.2 us  [the longest x1 8.1 us: body(): lax.all_to_all(back.reshape(N_EXP, 2 * CAP, COLS), EXPERT, split_axis=0,...]
  transfers between devices with their start and end apart: 8 -> 28, of which waited for: 6 -> 11; matrix products, arithmetic and copies ran while one was open for 27% -> 7% of each run, Pallas kernels for 0% -> 3%
where the time goes in v1:
time: 284 us; the launch traced here: 281 us
  waiting for transfers between devices  114 us (40%)
  starting transfers between devices  48.3 us (17%)
  Pallas kernels  47.9 us (17%)
  blocking collectives  29.8 us (10%)
  local copies, waits for them, and re-layouts  20 us (7%)
  between operations  16.9 us (6%)
  other arithmetic  3.6 us (1%)
    ppermute x24, waiting for transfers between devices, shift(): lax.ppermute(value, axis, [(i, (i + by) % size) for i in range(size)])  59.3 us
    reduce_scatter x1, waiting for transfers between devices, body(): sums = lax.psum_scatter(big, DP, scatter_dimension=0, tiled=False)  45.8 us
    ppermute x24, starting transfers between devices, shift(): lax.ppermute(value, axis, [(i, (i + by) % size) for i in range(size)])  36 us
    all_to_all x1, blocking collectives, body(): lax.all_to_all(send.reshape(N_EXP, 2 * CAP, COLS), EXPERT, split_axis=0,...  29.8 us
    pallas_call x1, Pallas kernels, body(): pl.pallas_call(expert_kernel, out_shape=(jax.ShapeDtypeStruct((N_DP, ROWS...  29.5 us
    unnamed x34, local copies, waits for them, and re-layouts  11.2 us
    all_to_all x1, waiting for transfers between devices, body(): lax.all_to_all(back.reshape(N_EXP, 2 * CAP, COLS), EXPERT, split_axis=0,...  9.27 us
    all_to_all x1, starting transfers between devices, body(): lax.all_to_all(back.reshape(N_EXP, 2 * CAP, COLS), EXPERT, split_axis=0,...  8.1 us
  transfers between devices with their start and end apart: 28, of which 11 were waited for; matrix products, arithmetic and copies ran while one was open for 7% of the time, Pallas kernels for 3%

profile of v1, /device:TPU:8, one launch (start us, length us, event | category | flops | bytes accessed | tf_op | source)
XLA Modules:
  0.0 281.0 jit_solution(8425756871966041605)
XLA Ops:
  7.2 1.4 copy.38.routes_ref
  8.6 1.4 copy.39.gates_ref
  10.6 3.8 %shard_map.121 = bf16[1280,256]{1,0:T(8,128)(2,1)} custom-call(s32[3]{0:T(128)} %pad_add_fusion.place_ref.refs_0_, s32[128,4]{1,0:T(8,128)} %copy.38.routes_ref, f32[128,4]{1,0:T(8,128)} %copy.39.gates_ref, s32[8,1280]{1,0:T(8,128)} %constant.87.clone.table_ref, bf16[128,2048]{1,0:T(8,128)(2,1)} %refs_16_.1, bf16[128,2048]{1,0:T(8,128)(2,1)} %refs_17_.1), custom_call_target="tpu_custom_call" | custom-call | tf_op jit(solution)/shard_map/pallas_call | solution.py:329
  14.5 29.8 %all_to_all.15 = bf16[32,40,256]{2,1,0:T(8,128)(2,1)} all-to-all(bf16[32,40,256]{2,1,0:T(8,128)(2,1)} %bitcast.27), channel_id=1, replica_groups=mesh['x'=4,'c'=2,'y'=4,'z'=8] {'y','z'}, dimensions={0} | all-to-all | bytes 1310720 | tf_op jit(solution)/shard_map/all_to_all | solution.py:336
  44.3 2.4 shard_map.122
  47.1 0.7 fusion.4
  47.8 2.6 collective-permute-start.2
  50.4 1.5 collective-permute-start.3
  51.9 2.9 %collective-permute-start = (bf16[640,128]{1,0:T(8,128)(2,1)S(1)}, bf16[640,128]{1,0:T(8,128)(2,1)S(1)}, u32[]{:S(2)}, u32[]{:S(2)}) collective-permute-start(bf16[640,128]{1,0:T(8,128)(2,1)S(1)} %get-tuple-element.19), channel_id=1, source_target_pairs={{0,1},{1,2},{2,3},{3,4},{4,5},{5,6},{6,7},{7,0},{8,9},{9,10},{10,1... | collective-permute-start | bytes 491528 | tf_op jit(solution)/shard_map/ppermute | solution.py:35
  55.2 4.7 %collective-permute-done.2 = bf16[640,128]{1,0:T(8,128)(2,1)S(1)} collective-permute-done((bf16[640,128]{1,0:T(8,128)(2,1)S(1)}, bf16[640,128]{1,0:T(8,128)(2,1)S(1)}, u32[]{:S(2)}, u32[]{:S(2)}) %collective-permute-start.2) | collective-permute-done | bytes 163872 | tf_op jit(solution)/shard_map/ppermute | solution.py:35
  59.9 1.7 collective-permute-start.6
  61.7 2.5 collective-permute-start.7
  64.1 1.2 collective-permute-start.4
  65.3 2.1 collective-permute-start.5
  67.4 0.7 constant_dynamic-update-slice_fusion.7
  68.1 0.7 constant_dynamic-update-slice_fusion.6
  68.7 0.7 constant_dynamic-update-slice_fusion.5
  69.4 0.7 constant_dynamic-update-slice_fusion.4
  70.7 0.7 constant_dynamic-update-slice_fusion.3
  71.4 0.7 constant_dynamic-update-slice_fusion.2
  72.0 0.6 constant_dynamic-update-slice_fusion.1
  72.7 0.6 constant_dynamic-update-slice_fusion.refs_1_
  73.3 1.5 collective-permute-start.8
  74.8 0.7 collective-permute-start.9
  75.5 0.7 fusion.3
  76.1 1.3 collective-permute-start.12
  77.5 1.9 collective-permute-start.13
  82.6 0.9 divide_reduce_fusion
  83.6 0.9 and_reduce_fusion
  84.6 19.6 %collective-permute-done.12 = bf16[416,128]{1,0:T(8,128)(2,1)S(1)} collective-permute-done((bf16[416,128]{1,0:T(8,128)(2,1)S(1)}, bf16[416,128]{1,0:T(8,128)(2,1)S(1)}, u32[]{:S(2)}, u32[]{:S(2)}) %collective-permute-start.12) | collective-permute-done | bytes 106528 | tf_op jit(solution)/shard_map/ppermute | solution.py:35
  104.2 1.2 collective-permute-start.14
  105.4 0.9 collective-permute-start.15
  106.3 0.7 constant_dynamic-update-slice_fusion.12
  107.0 0.6 constant_dynamic-update-slice_fusion.11
  107.6 0.7 collective-permute-done.14
  108.9 0.7 collective-permute-done.15
  109.6 0.6 constant_dynamic-update-slice_fusion.9.refs_6_
  110.2 1.3 collective-permute-start.18
  111.6 2.8 collective-permute-start.19
  114.9 2.7 collective-permute-start.17
  118.4 0.9 slice.63
  119.4 1.4 collective-permute-start.10
  120.8 0.9 slice.64
  121.7 11.9 %collective-permute-done.18.refs_9_ = bf16[1664,128]{1,0:T(8,128)(2,1)S(1)} collective-permute-done((bf16[1664,128]{1,0:T(8,128)(2,1)}, bf16[1664,128]{1,0:T(8,128)(2,1)S(1)}, u32[]{:S(2)}, u32[]{:S(2)}) %collective-permute-start.18) | collective-permute-done | bytes 426016 | tf_op jit(solution)/shard_map/ppermute | solution.py:35
  133.7 0.7 slice.68
  134.5 1.6 collective-permute-start.22
  136.1 4.4 %collective-permute-done.16.refs_7_ = bf16[1664,128]{1,0:T(8,128)(2,1)} collective-permute-done((bf16[1664,128]{1,0:T(8,128)(2,1)}, bf16[1664,128]{1,0:T(8,128)(2,1)}, u32[]{:S(2)}, u32[]{:S(2)}) %collective-permute-start.16) | collective-permute-done | bytes 426016 | tf_op jit(solution)/shard_map/ppermute | solution.py:35
  140.5 1.0 collective-permute-start.20
  141.5 2.3 collective-permute-start.21
  144.0 0.7 slice.69
  144.7 4.1 %collective-permute-done.22.refs_13_ = bf16[832,128]{1,0:T(8,128)(2,1)S(1)} collective-permute-done((bf16[832,128]{1,0:T(8,128)(2,1)}, bf16[832,128]{1,0:T(8,128)(2,1)S(1)}, u32[]{:S(2)}, u32[]{:S(2)}) %collective-permute-start.22) | collective-permute-done | bytes 213024 | tf_op jit(solution)/shard_map/ppermute | solution.py:35
  148.9 0.8 sub.37.refs_18_
  149.7 12.6 %collective-permute-done.23.refs_14_ = bf16[832,128]{1,0:T(8,128)(2,1)} collective-permute-done((bf16[832,128]{1,0:T(8,128)(2,1)}, bf16[832,128]{1,0:T(8,128)(2,1)}, u32[]{:S(2)}, u32[]{:S(2)}) %collective-permute-start.23) | collective-permute-done | bytes 213024 | tf_op jit(solution)/shard_map/ppermute | solution.py:35
  162.4 0.7 copy-done.7
  163.3 29.5 %shard_map.123 = (bf16[8,1536,256]{2,1,0:T(8,128)(2,1)}, bf16[8,96,640]{2,1,0:T(8,128)(2,1)}) custom-call(s32[3]{0:T(128)} %pad_add_fusion.place_ref.refs_0_, bf16[5120,128]{1,0:T(8,128)(2,1)} %constant_dynamic-update-slice_fusion.refs_1_, bf16[5120,128]{1,0:T(8,128)(2,1)} %copy-done.1, bf16[5120,128]{1,0:T(8,128)(2,1)} %copy-done.2, ...), custom_call_target="tpu_custom_call" | custom-call | tf_op jit(solution)/shard_map/pallas_call | solution.py:348
  192.8 4.1 %all-to-all-start.2 = ((bf16[8,96,640]{2,1,0:T(8,128)(2,1)}), bf16[8,96,640]{2,1,0:T(8,128)(2,1)S(1)}, u32[]{:S(2)}, u32[]{:S(2)}) async-start(bf16[8,96,640]{2,1,0:T(8,128)(2,1)} %get-tuple-element.10), calls=%async_computation.3 | async-start | bytes 1966080 | tf_op jit(solution)/shard_map/all_to_all | solution.py:387
  196.9 45.8 %reduce-scatter.2.cloned.1.call-done = bf16[1,1536,256]{2,1,0:T(8,128)(2,1)} async-done(((bf16[8,1536,256]{2,1,0:T(8,128)(2,1)}), bf16[1,1536,256]{2,1,0:T(8,128)(2,1)}) %reduce-scatter.2.cloned.1.call-update) | async-done | bytes 786448 | tf_op jit(solution)/shard_map/reduce_scatter | solution.py:367
  242.7 2.5 shard_map.124
  245.2 8.1 %all-to-all-start.1 = ((bf16[32,40,256]{2,1,0:T(8,128)(2,1)}), bf16[32,40,256]{2,1,0:T(8,128)(2,1)S(1)}, u32[]{:S(2)}, u32[]{:S(2)}) async-start(bf16[32,40,256]{2,1,0:T(8,128)(2,1)} %bitcast.25), calls=%async_computation.2 | async-start | bytes 1310720 | tf_op jit(solution)/shard_map/all_to_all | solution.py:376
  253.6 0.8 copy.40.code_ref
  254.3 6.5 %shard_map.126 = bf16[3,176,2048]{2,1,0:T(8,128)(2,1)} custom-call(s32[176,1]{1,0:T(8,128)} %copy.40.code_ref, bf16[8,96,640]{2,1,0:T(8,128)(2,1)} %copy-done, bf16[8,1280,256]{2,1,0:T(8,128)(2,1)} %bitcast.21), custom_call_target="tpu_custom_call" | custom-call | tf_op jit(solution)/shard_map/pallas_call | solution.py:388
  260.9 9.3 %all-to-all-done.1 = bf16[32,40,256]{2,1,0:T(8,128)(2,1)S(1)} async-done(((bf16[32,40,256]{2,1,0:T(8,128)(2,1)}), bf16[32,40,256]{2,1,0:T(8,128)(2,1)S(1)}, u32[]{:S(2)}, u32[]{:S(2)}) %all-to-all-start.1) | async-done | bytes 655392 | tf_op jit(solution)/shard_map/all_to_all | solution.py:376
  270.1 0.9 copy-done.3
  271.0 3.2 %shard_map.125 = (bf16[128,256]{1,0:T(8,128)(2,1)}, bf16[128,256]{1,0:T(8,128)(2,1)}) custom-call(s32[128,4]{1,0:T(8,128)} %copy.38.routes_ref, f32[128,4]{1,0:T(8,128)} %copy.39.gates_ref, s32[8,1280]{1,0:T(8,128)} %constant.87.clone.table_ref, bf16[1280,256]{1,0:T(8,128)(2,1)} %bitcast.24, bf16[1536,256]{1,0:T(8,128)(2,1)} %bitcast.23), custom_call_target="tpu_custom_call" | custom-call | tf_op jit(solution)/shard_map/pallas_call | solution.py:379
  (73 shorter events, 5.8 us)
Async XLA Ops:
  7.2 155.2 %all-gather.3.cloned.1.call-start = ((), (), s32[]{:S(2)}) async-start(), calls=%async_computation.5 | async-start | bytes 5898240 | tf_op jit(solution)/shard_map/all_gather | solution.py:346
  44.3 2.4 copy-start.8
  46.7 196.0 %reduce-scatter.2.cloned.1.call-start = ((), (), s32[]{:S(2)}) async-start(), calls=%async_computation.4 | async-start | bytes 7077888 | tf_op jit(solution)/shard_map/reduce_scatter | solution.py:367
  47.8 12.1 %collective-permute-start.2 = (bf16[640,128]{1,0:T(8,128)(2,1)S(1)}, bf16[640,128]{1,0:T(8,128)(2,1)S(1)}, u32[]{:S(2)}, u32[]{:S(2)}) collective-permute-start(bf16[640,128]{1,0:T(8,128)(2,1)S(1)} %get-tuple-element.19), channel_id=1, source_target_pairs={{0,2},{1,3},{2,4},{3,5},{4,6},{5,7},{6,0},{7,1},{8,10},{9,11},{10,... | collective-permute-start | bytes 491528 | tf_op jit(solution)/shard_map/ppermute | solution.py:35
  50.4 11.2 %collective-permute-start.3 = (bf16[640,128]{1,0:T(8,128)(2,1)S(1)}, bf16[640,128]{1,0:T(8,128)(2,1)S(1)}, u32[]{:S(2)}, u32[]{:S(2)}) collective-permute-start(bf16[640,128]{1,0:T(8,128)(2,1)S(1)} %get-tuple-element.19), channel_id=1, source_target_pairs={{0,6},{1,7},{2,0},{3,1},{4,2},{5,3},{6,4},{7,5},{8,14},{9,15},{10,... | collective-permute-start | bytes 491528 | tf_op jit(solution)/shard_map/ppermute | solution.py:35
  51.9 13.4 %collective-permute-start = (bf16[640,128]{1,0:T(8,128)(2,1)S(1)}, bf16[640,128]{1,0:T(8,128)(2,1)S(1)}, u32[]{:S(2)}, u32[]{:S(2)}) collective-permute-start(bf16[640,128]{1,0:T(8,128)(2,1)S(1)} %get-tuple-element.19), channel_id=1, source_target_pairs={{0,1},{1,2},{2,3},{3,4},{4,5},{5,6},{6,7},{7,0},{8,9},{9,10},{10,1... | collective-permute-start | bytes 491528 | tf_op jit(solution)/shard_map/ppermute | solution.py:35
  54.8 13.3 %collective-permute-start.1 = (bf16[640,128]{1,0:T(8,128)(2,1)S(1)}, bf16[640,128]{1,0:T(8,128)(2,1)S(1)}, u32[]{:S(2)}, u32[]{:S(2)}) collective-permute-start(bf16[640,128]{1,0:T(8,128)(2,1)S(1)} %get-tuple-element.19), channel_id=1, source_target_pairs={{0,7},{1,0},{2,1},{3,2},{4,3},{5,4},{6,5},{7,6},{8,15},{9,8},{10,9... | collective-permute-start | bytes 491528 | tf_op jit(solution)/shard_map/ppermute | solution.py:35
  59.9 12.1 %collective-permute-start.6 = (bf16[320,128]{1,0:T(8,128)(2,1)S(1)}, bf16[320,128]{1,0:T(8,128)(2,1)S(1)}, u32[]{:S(2)}, u32[]{:S(2)}) collective-permute-start(bf16[320,128]{1,0:T(8,128)(2,1)S(1)} %slice.61), channel_id=1, source_target_pairs={{0,2},{1,3},{2,4},{3,5},{4,6},{5,7},{6,0},{7,1},{8,10},{9,11},{10,... | collective-permute-start | bytes 245768 | tf_op jit(solution)/shard_map/ppermute | solution.py:35
  61.7 11.0 %collective-permute-start.7 = (bf16[320,128]{1,0:T(8,128)(2,1)S(1)}, bf16[320,128]{1,0:T(8,128)(2,1)S(1)}, u32[]{:S(2)}, u32[]{:S(2)}) collective-permute-start(bf16[320,128]{1,0:T(8,128)(2,1)S(1)} %slice.62), channel_id=1, source_target_pairs={{0,6},{1,7},{2,0},{3,1},{4,2},{5,3},{6,4},{7,5},{8,14},{9,15},{10,... | collective-permute-start | bytes 245768 | tf_op jit(solution)/shard_map/ppermute | solution.py:35
  64.1 6.5 %collective-permute-start.4 = (bf16[640,128]{1,0:T(8,128)(2,1)S(1)}, bf16[640,128]{1,0:T(8,128)(2,1)S(1)}, u32[]{:S(2)}, u32[]{:S(2)}) collective-permute-start(bf16[640,128]{1,0:T(8,128)(2,1)S(1)} %collective-permute-done.2), channel_id=1, source_target_pairs={{0,1},{1,2},{2,3},{3,4},{4,5},{5,6},{6,7},{7,0},{8,9},{9,10},{10,1... | collective-permute-start | bytes 491528 | tf_op jit(solution)/shard_map/ppermute | solution.py:35
  65.3 6.1 %collective-permute-start.5 = (bf16[640,128]{1,0:T(8,128)(2,1)S(1)}, bf16[640,128]{1,0:T(8,128)(2,1)S(1)}, u32[]{:S(2)}, u32[]{:S(2)}) collective-permute-start(bf16[640,128]{1,0:T(8,128)(2,1)S(1)} %collective-permute-done.3), channel_id=1, source_target_pairs={{0,7},{1,0},{2,1},{3,2},{4,3},{5,4},{6,5},{7,6},{8,15},{9,8},{10,9... | collective-permute-start | bytes 491528 | tf_op jit(solution)/shard_map/ppermute | solution.py:35
  67.4 12.0 %copy-start.10 = (s32[32]{0:T(128)S(1)}, s32[32]{0:T(128)}, u32[]{:S(2)}) copy-start(s32[32]{0:T(128)} %param.16) | copy-start | bytes 388
  73.3 41.6 %collective-permute-start.8 = (bf16[5120,128]{1,0:T(8,128)(2,1)}, bf16[5120,128]{1,0:T(8,128)(2,1)S(1)}, u32[]{:S(2)}, u32[]{:S(2)}) collective-permute-start(bf16[5120,128]{1,0:T(8,128)(2,1)} %constant_dynamic-update-slice_fusion.refs_1_), channel_id=1, source_target_pairs={{0,8},{8,16},{16,24},{24,0},{1,9},{9,17},{17,25},{25,1},{2,10},{10... | collective-permute-start | bytes 3932168 | tf_op jit(solution)/shard_map/ppermute | solution.py:35
  74.8 44.6 %collective-permute-start.9 = (bf16[5120,128]{1,0:T(8,128)(2,1)}, bf16[5120,128]{1,0:T(8,128)(2,1)S(1)}, u32[]{:S(2)}, u32[]{:S(2)}) collective-permute-start(bf16[5120,128]{1,0:T(8,128)(2,1)} %constant_dynamic-update-slice_fusion.refs_1_), channel_id=1, source_target_pairs={{0,24},{8,0},{16,8},{24,16},{1,25},{9,1},{17,9},{25,17},{2,26},{10... | collective-permute-start | bytes 3932168 | tf_op jit(solution)/shard_map/ppermute | solution.py:35
  76.1 28.0 %collective-permute-start.12 = (bf16[416,128]{1,0:T(8,128)(2,1)S(1)}, bf16[416,128]{1,0:T(8,128)(2,1)S(1)}, u32[]{:S(2)}, u32[]{:S(2)}) collective-permute-start(bf16[416,128]{1,0:T(8,128)(2,1)S(1)} %get-tuple-element.17), channel_id=1, source_target_pairs={{0,8},{8,16},{16,24},{24,0},{1,9},{9,17},{17,25},{25,1},{2,10},{10... | collective-permute-start | bytes 319496 | tf_op jit(solution)/shard_map/ppermute | solution.py:35
  77.5 27.9 %collective-permute-start.13 = (bf16[416,128]{1,0:T(8,128)(2,1)S(1)}, bf16[416,128]{1,0:T(8,128)(2,1)S(1)}, u32[]{:S(2)}, u32[]{:S(2)}) collective-permute-start(bf16[416,128]{1,0:T(8,128)(2,1)S(1)} %get-tuple-element.17), channel_id=1, source_target_pairs={{0,24},{8,0},{16,8},{24,16},{1,25},{9,1},{17,9},{25,17},{2,26},{10... | collective-permute-start | bytes 319496 | tf_op jit(solution)/shard_map/ppermute | solution.py:35
  104.2 4.1 %collective-permute-start.14 = (bf16[208,128]{1,0:T(8,128)(2,1)S(1)}, bf16[208,128]{1,0:T(8,128)(2,1)S(1)}, u32[]{:S(2)}, u32[]{:S(2)}) collective-permute-start(bf16[208,128]{1,0:T(8,128)(2,1)S(1)} %slice.66), channel_id=1, source_target_pairs={{0,8},{8,16},{16,24},{24,0},{1,9},{9,17},{17,25},{25,1},{2,10},{10... | collective-permute-start | bytes 159752 | tf_op jit(solution)/shard_map/ppermute | solution.py:35
  105.4 4.2 %collective-permute-start.15 = (bf16[208,128]{1,0:T(8,128)(2,1)S(1)}, bf16[208,128]{1,0:T(8,128)(2,1)S(1)}, u32[]{:S(2)}, u32[]{:S(2)}) collective-permute-start(bf16[208,128]{1,0:T(8,128)(2,1)S(1)} %slice.67), channel_id=1, source_target_pairs={{0,24},{8,0},{16,8},{24,16},{1,25},{9,1},{17,9},{25,17},{2,26},{10... | collective-permute-start | bytes 159752 | tf_op jit(solution)/shard_map/ppermute | solution.py:35
  110.2 23.4 %collective-permute-start.18 = (bf16[1664,128]{1,0:T(8,128)(2,1)}, bf16[1664,128]{1,0:T(8,128)(2,1)S(1)}, u32[]{:S(2)}, u32[]{:S(2)}) collective-permute-start(bf16[1664,128]{1,0:T(8,128)(2,1)} %constant_dynamic-update-slice_fusion.9.refs_6_), channel_id=1, source_target_pairs={{0,2},{1,3},{2,4},{3,5},{4,6},{5,7},{6,0},{7,1},{8,10},{9,11},{10,... | collective-permute-start | bytes 1277960 | tf_op jit(solution)/shard_map/ppermute | solution.py:35
  111.6 22.9 %collective-permute-start.19 = (bf16[1664,128]{1,0:T(8,128)(2,1)}, bf16[1664,128]{1,0:T(8,128)(2,1)S(1)}, u32[]{:S(2)}, u32[]{:S(2)}) collective-permute-start(bf16[1664,128]{1,0:T(8,128)(2,1)} %constant_dynamic-update-slice_fusion.9.refs_6_), channel_id=1, source_target_pairs={{0,6},{1,7},{2,0},{3,1},{4,2},{5,3},{6,4},{7,5},{8,14},{9,15},{10,... | collective-permute-start | bytes 1277960 | tf_op jit(solution)/shard_map/ppermute | solution.py:35
  114.4 26.1 %collective-permute-start.16 = (bf16[1664,128]{1,0:T(8,128)(2,1)}, bf16[1664,128]{1,0:T(8,128)(2,1)}, u32[]{:S(2)}, u32[]{:S(2)}) collective-permute-start(bf16[1664,128]{1,0:T(8,128)(2,1)} %constant_dynamic-update-slice_fusion.9.refs_6_), channel_id=1, source_target_pairs={{0,1},{1,2},{2,3},{3,4},{4,5},{5,6},{6,7},{7,0},{8,9},{9,10},{10,1... | collective-permute-start | bytes 1277960 | tf_op jit(solution)/shard_map/ppermute | solution.py:35
  114.9 6.8 %copy-start.1 = (bf16[5120,128]{1,0:T(8,128)(2,1)}, bf16[5120,128]{1,0:T(8,128)(2,1)S(1)}, u32[]{:S(2)}) copy-start(bf16[5120,128]{1,0:T(8,128)(2,1)S(1)} %collective-permute-done.8.refs_2_) | copy-start | bytes 3932164
  114.9 26.5 %collective-permute-start.17 = (bf16[1664,128]{1,0:T(8,128)(2,1)}, bf16[1664,128]{1,0:T(8,128)(2,1)}, u32[]{:S(2)}, u32[]{:S(2)}) collective-permute-start(bf16[1664,128]{1,0:T(8,128)(2,1)} %constant_dynamic-update-slice_fusion.9.refs_6_), channel_id=1, source_target_pairs={{0,7},{1,0},{2,1},{3,2},{4,3},{5,4},{6,5},{7,6},{8,15},{9,8},{10,9... | collective-permute-start | bytes 1277960 | tf_op jit(solution)/shard_map/ppermute | solution.py:35
  119.4 43.0 %copy-start.2 = (bf16[5120,128]{1,0:T(8,128)(2,1)}, bf16[5120,128]{1,0:T(8,128)(2,1)S(1)}, u32[]{:S(2)}) copy-start(bf16[5120,128]{1,0:T(8,128)(2,1)S(1)} %collective-permute-done.9.refs_3_) | copy-start | bytes 3932164
  119.4 43.0 %collective-permute-start.10 = (bf16[2560,128]{1,0:T(8,128)(2,1)}, bf16[2560,128]{1,0:T(8,128)(2,1)}, u32[]{:S(2)}, u32[]{:S(2)}) collective-permute-start(bf16[2560,128]{1,0:T(8,128)(2,1)} %slice.63), channel_id=1, source_target_pairs={{0,8},{8,16},{16,24},{24,0},{1,9},{9,17},{17,25},{25,1},{2,10},{10... | collective-permute-start | bytes 1966088 | tf_op jit(solution)/shard_map/ppermute | solution.py:35
  133.6 28.8 %copy-start.4 = (bf16[1664,128]{1,0:T(8,128)(2,1)}, bf16[1664,128]{1,0:T(8,128)(2,1)S(1)}, u32[]{:S(2)}) copy-start(bf16[1664,128]{1,0:T(8,128)(2,1)S(1)} %collective-permute-done.18.refs_9_) | copy-start | bytes 1277956
  133.6 28.7 %collective-permute-start.11 = (bf16[2560,128]{1,0:T(8,128)(2,1)}, bf16[2560,128]{1,0:T(8,128)(2,1)S(1)}, u32[]{:S(2)}, u32[]{:S(2)}) collective-permute-start(bf16[2560,128]{1,0:T(8,128)(2,1)} %slice.64), channel_id=1, source_target_pairs={{0,24},{8,0},{16,8},{24,16},{1,25},{9,1},{17,9},{25,17},{2,26},{10... | collective-permute-start | bytes 1966088 | tf_op jit(solution)/shard_map/ppermute | solution.py:35
  134.4 27.9 %copy-start.5 = (bf16[1664,128]{1,0:T(8,128)(2,1)}, bf16[1664,128]{1,0:T(8,128)(2,1)S(1)}, u32[]{:S(2)}) copy-start(bf16[1664,128]{1,0:T(8,128)(2,1)S(1)} %collective-permute-done.19.refs_10_) | copy-start | bytes 1277956
  134.5 14.4 %collective-permute-start.22 = (bf16[832,128]{1,0:T(8,128)(2,1)}, bf16[832,128]{1,0:T(8,128)(2,1)S(1)}, u32[]{:S(2)}, u32[]{:S(2)}) collective-permute-start(bf16[832,128]{1,0:T(8,128)(2,1)} %slice.68), channel_id=1, source_target_pairs={{0,2},{1,3},{2,4},{3,5},{4,6},{5,7},{6,0},{7,1},{8,10},{9,11},{10,... | collective-permute-start | bytes 638984 | tf_op jit(solution)/shard_map/ppermute | solution.py:35
  140.5 21.8 %collective-permute-start.20 = (bf16[1664,128]{1,0:T(8,128)(2,1)S(1)}, bf16[1664,128]{1,0:T(8,128)(2,1)S(1)}, u32[]{:S(2)}, u32[]{:S(2)}) collective-permute-start(bf16[1664,128]{1,0:T(8,128)(2,1)S(1)} %collective-permute-done.18.refs_9_), channel_id=1, source_target_pairs={{0,1},{1,2},{2,3},{3,4},{4,5},{5,6},{6,7},{7,0},{8,9},{9,10},{10,1... | collective-permute-start | bytes 1277960 | tf_op jit(solution)/shard_map/ppermute | solution.py:35
  141.5 20.8 %collective-permute-start.21 = (bf16[1664,128]{1,0:T(8,128)(2,1)S(1)}, bf16[1664,128]{1,0:T(8,128)(2,1)}, u32[]{:S(2)}, u32[]{:S(2)}) collective-permute-start(bf16[1664,128]{1,0:T(8,128)(2,1)S(1)} %collective-permute-done.19.refs_10_), channel_id=1, source_target_pairs={{0,7},{1,0},{2,1},{3,2},{4,3},{5,4},{6,5},{7,6},{8,15},{9,8},{10,9... | collective-permute-start | bytes 1277960 | tf_op jit(solution)/shard_map/ppermute | solution.py:35
  148.9 13.5 %copy-start.9 = (bf16[832,128]{1,0:T(8,128)(2,1)}, bf16[832,128]{1,0:T(8,128)(2,1)S(1)}, u32[]{:S(2)}) copy-start(bf16[832,128]{1,0:T(8,128)(2,1)S(1)} %collective-permute-done.22.refs_13_) | copy-start | bytes 638980
  148.9 13.4 %collective-permute-start.23 = (bf16[832,128]{1,0:T(8,128)(2,1)}, bf16[832,128]{1,0:T(8,128)(2,1)}, u32[]{:S(2)}, u32[]{:S(2)}) collective-permute-start(bf16[832,128]{1,0:T(8,128)(2,1)} %slice.69), channel_id=1, source_target_pairs={{0,6},{1,7},{2,0},{3,1},{4,2},{5,3},{6,4},{7,5},{8,14},{9,15},{10,... | collective-permute-start | bytes 638984 | tf_op jit(solution)/shard_map/ppermute | solution.py:35
  162.3 0.8 copy-start.7
  162.3 1.0 copy-start.6
  192.8 52.4 %all-to-all-start.2 = ((bf16[8,96,640]{2,1,0:T(8,128)(2,1)}), bf16[8,96,640]{2,1,0:T(8,128)(2,1)S(1)}, u32[]{:S(2)}, u32[]{:S(2)}) async-start(bf16[8,96,640]{2,1,0:T(8,128)(2,1)} %get-tuple-element.10), calls=%async_computation.3 | async-start | bytes 1966080 | tf_op jit(solution)/shard_map/all_to_all | solution.py:387
  245.2 9.1 %copy-start = (bf16[8,96,640]{2,1,0:T(8,128)(2,1)}, bf16[8,96,640]{2,1,0:T(8,128)(2,1)S(1)}, u32[]{:S(2)}) copy-start(bf16[8,96,640]{2,1,0:T(8,128)(2,1)S(1)} %all-to-all-done.2.acts_ref) | copy-start | bytes 2949124
  245.2 24.9 %all-to-all-start.1 = ((bf16[32,40,256]{2,1,0:T(8,128)(2,1)}), bf16[32,40,256]{2,1,0:T(8,128)(2,1)S(1)}, u32[]{:S(2)}, u32[]{:S(2)}) async-start(bf16[32,40,256]{2,1,0:T(8,128)(2,1)} %bitcast.25), calls=%async_computation.2 | async-start | bytes 1310720 | tf_op jit(solution)/shard_map/all_to_all | solution.py:376
  270.1 0.9 copy-start.3
Sparse Core Ops, SparseCore 0:
  46.8 37.4 all-gather.2
  193.0 49.6 reduce-scatter.1

commit v2 on v1

--- a/solution.py
+++ b/solution.py
@@ -22,7 +22,9 @@
 SLOTS = N_EXP * CAP
 ROWS = 2 * SLOTS
 COLS = D // N_DP
-PART_A = 640
+SUM_ROWS = SLOTS + TOK
+SUM_HALF = SUM_ROWS // 2
+PART_A = 512
 PART_B = 3 * HALF - PART_A
 F32, BF16 = jnp.float32, jnp.bfloat16
 VMEM_LIMIT = 60 * 1024 * 1024
@@ -142,24 +144,51 @@
         out_ref[SLOTS + 80 * b : SLOTS + 80 * (b + 1), :] = rows[80:]
 
 
-def order_out_kernel(order_ref, in_ref, out_ref):
+def sum_pair_kernel(keep_ref, got_ref, own_ref, next_ref, last_ref, far_up_ref, far_down_ref):
+    def total(i, rows=slice(None)):
+        return (keep_ref[i, rows].astype(F32) + got_ref[i, rows].astype(F32)).astype(BF16)
+
+    own_ref[...] = total(0)
+    next_ref[...] = total(1)
+    last_ref[...] = total(3)
+    far_up_ref[...] = total(2, slice(0, SUM_HALF))
+    far_down_ref[...] = total(2, slice(SUM_HALF, SUM_ROWS))
+
+
+def sum_far_kernel(next_ref, last_ref, up_ref, down_ref, next_out, last_out):
+    top, bottom = slice(0, SUM_HALF), slice(SUM_HALF, SUM_ROWS)
+    next_out[top] = (next_ref[top].astype(F32) + up_ref[...].astype(F32)).astype(BF16)
+    next_out[bottom] = next_ref[bottom]
+    last_out[top] = last_ref[top]
+    last_out[bottom] = (last_ref[bottom].astype(F32) + down_ref[...].astype(F32)).astype(BF16)
+
+
+def sum_last_kernel(*refs):
+    order_ref, out_refs, back_refs = refs[0], refs[1:4], refs[4:7]
+    rows_ref, own_ref = refs[7:]
+
+    def total(parts, rows):
+        return sum(part[rows].astype(F32) for part in parts)
+
     for b in range(8):
-        rows = jnp.concatenate(
-            [in_ref[80 * b : 80 * (b + 1), :], in_ref[SLOTS + 80 * b : SLOTS + 80 * (b + 1), :]],
-            axis=0,
-        )
-        out_ref[160 * b : 160 * (b + 1), :] = dot_first(order_ref[...], rows).astype(BF16)
-
-
-def combine_kernel(routes_ref, gates_ref, table_ref, back_ref, sums_ref, mixed_ref, grad_ref):
+        rows = slice(80 * b, 80 * (b + 1))
+        both = jnp.concatenate([total(out_refs, rows), total(back_refs, rows)], axis=0)
+        rows_ref[160 * b : 160 * (b + 1), :] = dot_first(
+            order_ref[...], both.astype(BF16)
+        ).astype(BF16)
+    rows = slice(SLOTS, SLOTS + TOK)
+    own_ref[0] = total(out_refs, rows)
+    own_ref[1] = total(back_refs, rows)
+
+
+def combine_kernel(routes_ref, gates_ref, table_ref, back_ref, own_ref, mixed_ref, grad_ref):
     first, second, gate = slot_masks(routes_ref, gates_ref, table_ref)
     rows = back_ref[...]
-    mixed = sums_ref[ROWS : ROWS + TOK, :].astype(F32)
+    mixed = own_ref[0]
     for piece in split3(first * gate):
         mixed = mixed + dot(piece, rows)
     mixed_ref[...] = mixed.astype(BF16)
-    grad = sums_ref[ROWS + TOK : ROWS + 2 * TOK, :].astype(F32) + dot(second.astype(BF16), rows)
-    grad_ref[...] = grad.astype(BF16)
+    grad_ref[...] = (own_ref[1] + dot(second.astype(BF16), rows)).astype(BF16)
 
 
 def block_copies(refs, gathered, place_ref, sems):
@@ -171,17 +200,17 @@
         e = lax.rem(device_y + 2 * NY, NY) * NZ + lax.rem(device_z + 2 * NZ, NZ)
         copies.append(
             pltpu.make_async_copy(
-                source, gathered.at[e, pl.ds(start, count)], sems.at[len(copies) % 8]
+                source, gathered.at[e, pl.ds(start, count)], sems.at[0 if start == 0 else 1, e]
             )
         )
 
     for i, dy in enumerate(Y_FROM):
-        for j, dz in enumerate(Z_FROM):
+        for j in range(NZ):
             if i < 3:
                 source = a_refs[i].at[pl.ds(j * PART_A, PART_A)]
             else:
                 source = a_refs[3 + j // 4].at[pl.ds(j % 4 * PART_A, PART_A)]
-            add(source, y + dy, z + dz, 0, PART_A)
+            add(source, y + dy, j, 0, PART_A)
     for j, dz in enumerate(Z_FROM):
         for i, dy in enumerate(Y_FROM):
             if j < 7:
@@ -196,8 +225,8 @@
     place_ref = refs[0]
     pieces = refs[1:15]
     rows_ref, tokens_ref, cot_ref, pick_ref, pair_ref = refs[15:20]
-    big_ref, acts_ref = refs[20:22]
-    gathered, weights, rows, picked, sems, row_sems = refs[22:]
+    sum_refs, acts_ref = refs[20:24], refs[24]
+    gathered, weights, rows, picked, sums, sems, row_sems, sum_sems = refs[25:]
     copies = block_copies(pieces, gathered, place_ref, sems)
     row_copies = [
         pltpu.make_async_copy(
@@ -209,14 +238,16 @@
         copy.start()
     unit = lax.broadcasted_iota(jnp.int32, (N_DP * PAD, UNITS), 1)
     pick = jnp.where(pick_ref[...] == unit, 1.0, 0.0).astype(BF16)
-    for copy in copies:
-        copy.wait()
 
     def assemble(g, carry):
+        for i in range(4):
+            for k, (start, count) in enumerate(((0, PART_A), (PART_A, PART_B))):
+                block = gathered.at[4 * g + i, pl.ds(start, count)]
+                pltpu.make_async_copy(block, block, sems.at[k, 4 * g + i]).wait()
         for half in range(2):
             j = 2 * g + half
-            both = jnp.concatenate([gathered[2 * j], gathered[2 * j + 1]], axis=1)
-            mixed = dot(both, pair_ref[...]).astype(BF16)
+            low, high = gathered[2 * j], gathered[2 * j + 1]
+            mixed = jnp.concatenate([low[:, :64], high[:, :64], low[:, 64:], high[:, 64:]], axis=1)
             lanes = pl.ds(pl.multiple_of(j * 128, 128), 128)
             for m in range(3):
                 part = mixed[m * HALF : (m + 1) * HALF]
@@ -227,7 +258,7 @@
             picked[m, :, lanes] = dot(pick, weights[m, :, lanes]).astype(BF16)
         return carry
 
-    lax.fori_loop(0, N_DP, assemble, 0)
+    lax.fori_loop(0, N_DP, assemble, 0, unroll=2)
 
     shared_gate = dot_last(tokens_ref[...], weights[0])
     shared_up = dot_last(tokens_ref[...], weights[1])
@@ -254,19 +285,34 @@
         for s in range(N_DP):
             acts_ref[s, m * PAD : (m + 1) * PAD, :] = value[s * PAD : (s + 1) * PAD]
 
-    def outputs(g, carry):
-        lanes = pl.ds(pl.multiple_of(g * COLS, COLS), COLS)
-        big_ref[g, :SLOTS, :] = dot(hidden_t, picked[2, :, lanes]).astype(BF16)
-        big_ref[g, SLOTS:ROWS, :] = (
-            dot(dgate_t, picked[0, :, lanes]) + dot(dup_t, picked[1, :, lanes])
-        ).astype(BF16)
-        big_ref[g, ROWS : ROWS + TOK, :] = dot(shared_hidden, weights[2, :, lanes]).astype(BF16)
-        big_ref[g, ROWS + TOK :, :] = (
-            dot(shared_dgate, weights[0, :, lanes]) + dot(shared_dup, weights[1, :, lanes])
-        ).astype(BF16)
+    x, c = place_ref[0] // NC, place_ref[0] % NC
+
+    def sum_copy(part, k, i):
+        return pltpu.make_async_copy(
+            sums.at[part, k, i], sum_refs[2 * part + k].at[i], sum_sems.at[part, k, i]
+        )
+
+    def outputs(i, carry):
+        for k in range(NC):
+            g = lax.rem(x + i, NX) * NC + (c if k == 0 else 1 - c)
+            lanes = pl.ds(pl.multiple_of(g * COLS, COLS), COLS)
+            sums[0, k, i, :SLOTS, :] = dot(hidden_t, picked[2, :, lanes]).astype(BF16)
+            sums[0, k, i, SLOTS:, :] = dot(shared_hidden, weights[2, :, lanes]).astype(BF16)
+            sum_copy(0, k, i).start()
+            sums[1, k, i, :SLOTS, :] = (
+                dot(dgate_t, picked[0, :, lanes]) + dot(dup_t, picked[1, :, lanes])
+            ).astype(BF16)
+            sums[1, k, i, SLOTS:, :] = (
+                dot(shared_dgate, weights[0, :, lanes]) + dot(shared_dup, weights[1, :, lanes])
+            ).astype(BF16)
+            sum_copy(1, k, i).start()
         return carry
 
-    lax.fori_loop(0, N_DP, outputs, 0)
+    lax.fori_loop(0, NX, outputs, 0)
+    for part in range(2):
+        for k in range(NC):
+            for i in range(NX):
+                sum_copy(part, k, i).wait()
 
 
 def grad_kernel(code_ref, acts_ref, rows_ref, out_ref):
@@ -284,32 +330,38 @@
             ).astype(BF16)
 
 
-def gather_weights(dense_weights):
+def stack_kernel(*refs):
+    sources, target = refs[:5], refs[5]
+    start = 0
+    for source in sources:
+        count = source.shape[0]
+        target[start : start + count, :] = source[...]
+        start += count
+
+
+def tie(values, *others):
+    return lax.optimization_barrier((tuple(values),) + others)
+
+
+def pack_weights(dense_weights):
     packed = jnp.concatenate([dense_weights[:, :HALF], dense_weights[:, HALF:]], axis=2)
-    packed = packed.reshape(3 * HALF, 128)
-
-    def along_z(own):
-        half = own.shape[0] // 2
-        f1, b1 = shift(own, "z", 1), shift(own, "z", -1)
-        f2, b2 = shift(own, "z", 2), shift(own, "z", -2)
-        f3, b3 = shift(f2, "z", 1), shift(b2, "z", -1)
-        return [own, f1, b1, f2, b2, f3, b3, shift(f2[:half], "z", 2), shift(b2[half:], "z", -2)]
-
-    def along_y(own):
-        half = own.shape[0] // 2
-        f, b = shift(own, "y", 1), shift(own, "y", -1)
-        return [own, f, b, shift(f[:half], "y", 1), shift(b[half:], "y", -1)]
-
-    part_a = along_y(jnp.concatenate(along_z(packed[:PART_A])))
-    part_b = along_z(jnp.concatenate(along_y(packed[PART_A:])))
-    return part_a + part_b
+    return packed.reshape(3 * HALF, 128)
+
+
+def ends_two(own, axis, by):
+    f2, b2 = own
+    half = f2.shape[0] // 2
+    return shift(f2[:half], axis, by), shift(b2[half:], axis, -by)
 
 
 def body(dense_weights, tokens, cotangent, routes, route_gates, unit_perm, slab_owner):
     g = lax.axis_index(DP)
     y, z = lax.axis_index("y"), lax.axis_index("z")
     place = jnp.stack([g, y, z]).astype(jnp.int32)
-    pieces = gather_weights(dense_weights)
+    packed = pack_weights(dense_weights)
+    a0, b0 = packed[:PART_A], packed[PART_A:]
+    part_a = lax.all_gather(a0, "z", axis=0, tiled=True)
+    b_f, b_b = shift(b0, "y", 1), shift(b0, "y", -1)
 
     owned = slab_owner[y * NZ + z]
     units = lax.dynamic_slice(unit_perm, (owned // 4, owned % 4 * EH), (1, EH)).reshape(N_DP, SHARE)
@@ -336,6 +388,23 @@
     received = lax.all_to_all(
         send.reshape(N_EXP, 2 * CAP, COLS), EXPERT, split_axis=0, concat_axis=0, tiled=True
     ).reshape(ROWS, COLS)
+    part_b = pl.pallas_call(
+        stack_kernel,
+        out_shape=jax.ShapeDtypeStruct((NY * PART_B, 128), BF16),
+        in_specs=[vmem()] * 5,
+        out_specs=vmem(),
+        compiler_params=params(),
+    )(b0, b_f, b_b, *ends_two((b_f, b_b), "y", 1))
+    part_a, _ = lax.optimization_barrier((part_a, received))
+    received, _ = lax.optimization_barrier((received, part_b))
+    a_f, a_b = shift(part_a, "y", 1), shift(part_a, "y", -1)
+    b_f1, b_b1 = shift(part_b, "z", 1), shift(part_b, "z", -1)
+    b_f2, b_b2 = shift(b_f1, "z", 1), shift(b_b1, "z", -1)
+    b_f3, b_b3 = shift(b_f2, "z", 1), shift(b_b2, "z", -1)
+    pieces_b = [part_b, b_f1, b_b1, b_f2, b_b2, b_f3, b_b3]
+    a_f, a_b, b_f2, b_b2 = lax.optimization_barrier((a_f, a_b, b_f2, b_b2))
+    pieces = [part_a, a_f, a_b, *ends_two((a_f, a_b), "y", 1)] + pieces_b
+    pieces += ends_two((b_f3, b_b3), "z", 1)
     ordered = pl.pallas_call(
         order_in_kernel,
         out_shape=jax.ShapeDtypeStruct((ROWS, COLS), BF16),
@@ -345,34 +414,57 @@
     )(order, received)
     rows = lax.all_gather(ordered, DP, axis=0, tiled=False)
 
-    big, acts = pl.pallas_call(
+    keep_out, give_out, keep_back, give_back, acts = pl.pallas_call(
         expert_kernel,
-        out_shape=(
-            jax.ShapeDtypeStruct((N_DP, ROWS + 2 * TOK, COLS), BF16),
+        out_shape=(jax.ShapeDtypeStruct((NX, SUM_ROWS, COLS), BF16),) * 4
+        + (
             jax.ShapeDtypeStruct((N_DP, 3 * PAD, SLOTS), BF16),
         ),
         in_specs=[smem()] + [hbm()] * 15 + [vmem()] * 4,
-        out_specs=(vmem(), vmem()),
+        out_specs=(hbm(),) * 4 + (vmem(),),
         scratch_shapes=[
             pltpu.VMEM((N_EXP, 3 * HALF, 128), BF16),
             pltpu.VMEM((3, UNITS, D), BF16),
             pltpu.VMEM((ROWS, D), BF16),
             pltpu.VMEM((3, N_DP * PAD, D), BF16),
-            pltpu.SemaphoreType.DMA((8,)),
+            pltpu.VMEM((2, NC, NX, SUM_ROWS, COLS), BF16),
+            pltpu.SemaphoreType.DMA((2, N_EXP)),
             pltpu.SemaphoreType.DMA((N_DP,)),
+            pltpu.SemaphoreType.DMA((2, NC, NX)),
         ],
         compiler_params=params(),
     )(place, *pieces, rows, tokens, cotangent, pick, pair_matrix())
 
-    sums = lax.psum_scatter(big, DP, scatter_dimension=0, tiled=False)
-    sums = sums.reshape(ROWS + 2 * TOK, COLS)
-    back = pl.pallas_call(
-        order_out_kernel,
-        out_shape=jax.ShapeDtypeStruct((ROWS, COLS), BF16),
-        in_specs=[vmem()] * 2,
-        out_specs=vmem(),
-        compiler_params=params(),
-    )(order, sums)
+    def local(kernel, shapes, *values):
+        return pl.pallas_call(
+            kernel,
+            out_shape=tuple(jax.ShapeDtypeStruct(*shape) for shape in shapes),
+            in_specs=[vmem()] * len(values),
+            out_specs=(vmem(),) * len(shapes),
+            compiler_params=params(),
+        )(*values)
+
+    whole, half = ((SUM_ROWS, COLS), BF16), ((SUM_HALF, COLS), BF16)
+
+    def near(keep, got):
+        return local(sum_pair_kernel, [whole] * 3 + [half] * 2, keep, got)
+
+    def far(parts):
+        own, following, last, up, down = parts
+        following, last = local(
+            sum_far_kernel, [whole] * 2, following, last, shift(up, "x", 1), shift(down, "x", -1)
+        )
+        return own, shift(following, "x", 1), shift(last, "x", -1)
+
+    out_parts = far(near(keep_out, shift(give_out, "c", 1)))
+    back_parts = far(near(keep_back, shift(give_back, "c", 1)))
+    back, own = local(
+        sum_last_kernel,
+        [((ROWS, COLS), BF16), ((2, TOK, COLS), F32)],
+        order,
+        *out_parts,
+        *back_parts,
+    )
     back = lax.all_to_all(
         back.reshape(N_EXP, 2 * CAP, COLS), EXPERT, split_axis=0, concat_axis=0, tiled=True
     ).reshape(ROWS, COLS)
@@ -382,7 +474,7 @@
         in_specs=[vmem()] * 5,
         out_specs=(vmem(), vmem()),
         compiler_params=params(),
-    )(routes, route_gates, table, back, sums)
+    )(routes, route_gates, table, back, own)
 
     acts = lax.all_to_all(acts, DP, split_axis=0, concat_axis=0, tiled=True)
     grads = pl.pallas_call(

time: 284 us -> 224 us (0.79)
  waiting for transfers between devices: 114 us -> 63.9 us
  blocking collectives: 29.8 us -> 0 us
  starting transfers between devices: 48.3 us -> 64 us
  Pallas kernels: 47.9 us -> 57 us
  local copies, waits for them, and re-layouts: 20 us -> 15.6 us
    reduce_scatter x1 -> x0, waiting for transfers between devices: 45.8 us -> none  [body(): sums = lax.psum_scatter(big, DP, scatter_dimension=0, tiled=False)]
    all_to_all x1 -> x0, blocking collectives: 29.8 us -> none  [body(): lax.all_to_all(send.reshape(N_EXP, 2 * CAP, COLS), EXPERT, split_axis=0,...]
    ppermute x24 -> x26, waiting for transfers between devices: 59.3 us -> 46.5 us  [shift(): lax.ppermute(value, axis, [(i, (i + by) % size) for i in range(size)])]
    all_to_all x0 -> x1, starting transfers between devices: none -> 11.7 us  [body(): lax.all_to_all(send.reshape(N_EXP, 2 * CAP, COLS), EXPERT, split_axis=0,...]
    pallas_call x2 -> x7, Pallas kernels: 32 us -> 41.3 us  [the longest x1 25.6 us: body(): pl.pallas_call(expert_kernel, out_shape=(jax.ShapeDtypeStruct((NX, SUM_RO...]
    all_to_all x0 -> x1, waiting for transfers between devices: none -> 8.4 us  [body(): lax.all_to_all(send.reshape(N_EXP, 2 * CAP, COLS), EXPERT, split_axis=0,...]
    all_to_all x1, starting transfers between devices: 8.1 us -> 12.2 us  [body(): lax.all_to_all(back.reshape(N_EXP, 2 * CAP, COLS), EXPERT, split_axis=0,...]
    unnamed x34 -> x56, local copies, waits for them, and re-layouts: 11.2 us -> 7.67 us
  transfers between devices with their start and end apart: 28 -> 31, of which waited for: 11 -> 14; matrix products, arithmetic and copies ran while one was open for 7% -> 5% of each run, Pallas kernels for 3% -> 13%
where the time goes in v2:
time: 224 us; the launch traced here: 221 us
  starting transfers between devices  64 us (29%)
  waiting for transfers between devices  63.9 us (29%)
  Pallas kernels  57 us (25%)
  between operations  17 us (8%)
  local copies, waits for them, and re-layouts  15.6 us (7%)
  other arithmetic  3.64 us (2%)
    ppermute x26, waiting for transfers between devices, shift(): lax.ppermute(value, axis, [(i, (i + by) % size) for i in range(size)])  46.5 us
    ppermute x26, starting transfers between devices, shift(): lax.ppermute(value, axis, [(i, (i + by) % size) for i in range(size)])  35.5 us
    pallas_call x1, Pallas kernels, body(): pl.pallas_call(expert_kernel, out_shape=(jax.ShapeDtypeStruct((NX, SUM_RO...  25.6 us
    pallas_call x5, Pallas kernels, local(): pl.pallas_call(kernel, out_shape=tuple((jax.ShapeDtypeStruct(*shape) for...  13.7 us
    all_to_all x1, starting transfers between devices, body(): lax.all_to_all(back.reshape(N_EXP, 2 * CAP, COLS), EXPERT, split_axis=0,...  12.2 us
    all_to_all x1, starting transfers between devices, body(): lax.all_to_all(send.reshape(N_EXP, 2 * CAP, COLS), EXPERT, split_axis=0,...  11.7 us
    all_to_all x1, waiting for transfers between devices, body(): lax.all_to_all(back.reshape(N_EXP, 2 * CAP, COLS), EXPERT, split_axis=0,...  8.8 us
    all_to_all x1, waiting for transfers between devices, body(): lax.all_to_all(send.reshape(N_EXP, 2 * CAP, COLS), EXPERT, split_axis=0,...  8.4 us
  transfers between devices with their start and end apart: 31, of which 14 were waited for; matrix products, arithmetic and copies ran while one was open for 5% of the time, Pallas kernels for 13%

profile of v2, /device:TPU:8, one launch (start us, length us, event | category | flops | bytes accessed | tf_op | source)
XLA Modules:
  0.0 221.2 jit_solution(11636006247896142348)
XLA Ops:
  7.2 1.1 fusion.2
  8.6 0.7 slice.52
  9.3 0.7 copy.38.routes_ref
  10.0 0.7 copy.39.gates_ref
  10.8 0.6 pad_add_fusion.place_ref.refs_0_
  11.4 3.8 %shard_map.121 = bf16[1280,256]{1,0:T(8,128)(2,1)} custom-call(s32[3]{0:T(128)} %pad_add_fusion.place_ref.refs_0_, s32[128,4]{1,0:T(8,128)} %copy.38.routes_ref, f32[128,4]{1,0:T(8,128)} %copy.39.gates_ref, s32[8,1280]{1,0:T(8,128)} %constant.87.clone.table_ref, bf16[128,2048]{1,0:T(8,128)(2,1)} %refs_16_.1, bf16[128,2048]{1,0:T(8,128)(2,1)} %refs_17_.1), custom_call_target="tpu_custom_call" | custom-call | tf_op jit(solution)/shard_map/pallas_call | solution.py:381
  15.2 11.7 %all-to-all-start = ((bf16[32,40,256]{2,1,0:T(8,128)(2,1)}), bf16[32,40,256]{2,1,0:T(8,128)(2,1)S(1)}, u32[]{:S(2)}, u32[]{:S(2)}) async-start(bf16[32,40,256]{2,1,0:T(8,128)(2,1)} %bitcast.22), calls=%async_computation | async-start | bytes 1310720 | tf_op jit(solution)/shard_map/all_to_all | solution.py:388
  27.0 1.5 collective-permute-start.2
  29.1 4.1 %collective-permute-done.2.refs_1_ = bf16[544,128]{1,0:T(8,128)(2,1)S(1)} collective-permute-done((bf16[544,128]{1,0:T(8,128)(2,1)S(1)}, bf16[544,128]{1,0:T(8,128)(2,1)S(1)}, u32[]{:S(2)}, u32[]{:S(2)}) %collective-permute-start.2) | collective-permute-done | bytes 139296 | tf_op jit(solution)/shard_map/ppermute | solution.py:37
  33.2 1.7 collective-permute-start.4
  35.5 2.4 %collective-permute-done.4.refs_3_ = bf16[272,128]{1,0:T(8,128)(2,1)S(1)} collective-permute-done((bf16[272,128]{1,0:T(8,128)(2,1)S(1)}, bf16[272,128]{1,0:T(8,128)(2,1)S(1)}, u32[]{:S(2)}, u32[]{:S(2)}) %collective-permute-start.4) | collective-permute-done | bytes 69664 | tf_op jit(solution)/shard_map/ppermute | solution.py:37
  37.9 1.7 collective-permute-done.5.refs_4_
  39.6 0.6 copy-done.23
  40.3 2.0 shard_map.122.refs_6_
  42.2 8.4 %all-to-all-done = bf16[32,40,256]{2,1,0:T(8,128)(2,1)S(1)} async-done(((bf16[32,40,256]{2,1,0:T(8,128)(2,1)}), bf16[32,40,256]{2,1,0:T(8,128)(2,1)S(1)}, u32[]{:S(2)}, u32[]{:S(2)}) %all-to-all-start) | async-done | bytes 655392 | tf_op jit(solution)/shard_map/all_to_all | solution.py:388
  50.6 0.8 copy-done.1
  51.5 2.3 %shard_map.123 = bf16[1280,256]{1,0:T(8,128)(2,1)} custom-call(bf16[160,160]{1,0:T(8,128)(2,1)} %constant.88.clone.order_ref.refs_0_, bf16[1280,256]{1,0:T(8,128)(2,1)} %bitcast.21), custom_call_target="tpu_custom_call" | custom-call | tf_op jit(solution)/shard_map/pallas_call | solution.py:408
  53.8 2.2 collective-permute-start.6
  56.0 1.1 collective-permute-start.8
  57.3 1.2 collective-permute-start
  58.4 1.4 collective-permute-start.1
  59.8 8.6 %collective-permute-done.6.refs_7_ = bf16[2176,128]{1,0:T(8,128)(2,1)S(1)} collective-permute-done((bf16[2176,128]{1,0:T(8,128)(2,1)S(1)}, bf16[2176,128]{1,0:T(8,128)(2,1)S(1)}, u32[]{:S(2)}, u32[]{:S(2)}) %collective-permute-start.6) | collective-permute-done | bytes 557088 | tf_op jit(solution)/shard_map/ppermute | solution.py:37
  68.4 1.2 collective-permute-start.7
  69.6 2.0 collective-permute-start.9
  74.8 0.9 divide_reduce_fusion
  75.9 0.9 and_reduce_fusion
  76.9 0.6 reduce-window.6
  77.5 4.6 %collective-permute-done.7.refs_9_ = bf16[2176,128]{1,0:T(8,128)(2,1)} collective-permute-done((bf16[2176,128]{1,0:T(8,128)(2,1)S(1)}, bf16[2176,128]{1,0:T(8,128)(2,1)}, u32[]{:S(2)}, u32[]{:S(2)}) %collective-permute-start.7) | collective-permute-done | bytes 557088 | tf_op jit(solution)/shard_map/ppermute | solution.py:37
  82.6 2.7 %collective-permute-start.13 = (bf16[2176,128]{1,0:T(8,128)(2,1)}, bf16[2176,128]{1,0:T(8,128)(2,1)S(1)}, u32[]{:S(2)}, u32[]{:S(2)}) collective-permute-start(bf16[2176,128]{1,0:T(8,128)(2,1)} %collective-permute-done.9.refs_10_), channel_id=1, source_target_pairs={{0,7},{1,0},{2,1},{3,2},{4,3},{5,4},{6,5},{7,6},{8,15},{9,8},{10,9... | collective-permute-start | bytes 1671176 | tf_op jit(solution)/shard_map/ppermute | solution.py:37
  85.8 0.9 slice.45
  86.7 1.4 collective-permute-start.10
  88.1 0.8 slice.46
  89.6 5.4 %collective-permute-done.12.refs_11_ = bf16[2176,128]{1,0:T(8,128)(2,1)S(1)} collective-permute-done((bf16[2176,128]{1,0:T(8,128)(2,1)}, bf16[2176,128]{1,0:T(8,128)(2,1)S(1)}, u32[]{:S(2)}, u32[]{:S(2)}) %collective-permute-start.12) | collective-permute-done | bytes 557088 | tf_op jit(solution)/shard_map/ppermute | solution.py:37
  95.0 0.8 slice.56
  95.8 0.8 slice.57
  96.5 3.2 %collective-permute-start.15 = (bf16[1088,128]{1,0:T(8,128)(2,1)}, bf16[1088,128]{1,0:T(8,128)(2,1)}, u32[]{:S(2)}, u32[]{:S(2)}) collective-permute-start(bf16[1088,128]{1,0:T(8,128)(2,1)} %slice.57), channel_id=1, source_target_pairs={{0,7},{1,0},{2,1},{3,2},{4,3},{5,4},{6,5},{7,6},{8,15},{9,8},{10,9... | collective-permute-start | bytes 835592 | tf_op jit(solution)/shard_map/ppermute | solution.py:37
  100.0 0.8 sub.37.refs_18_
  100.8 3.0 %collective-permute-done.14.refs_13_ = bf16[1088,128]{1,0:T(8,128)(2,1)S(1)} collective-permute-done((bf16[1088,128]{1,0:T(8,128)(2,1)}, bf16[1088,128]{1,0:T(8,128)(2,1)S(1)}, u32[]{:S(2)}, u32[]{:S(2)}) %collective-permute-start.14) | collective-permute-done | bytes 278560 | tf_op jit(solution)/shard_map/ppermute | solution.py:37
  104.4 25.6 %shard_map.124 = (bf16[4,768,256]{2,1,0:T(8,128)(2,1)}, bf16[4,768,256]{2,1,0:T(8,128)(2,1)}, bf16[4,768,256]{2,1,0:T(8,128)(2,1)}, bf16[4,768,256]{2,1,0:T(8,128)(2,1)}, bf16[8,96,640]{2,1,0:T(8,128)(2,1)}) custom-call(s32[3]{0:T(128)} %pad_add_fusion.place_ref.refs_0_, bf16[4096,128]{1,0:T(8,128)(2,1)} %all-gather.4.cloned.1.call-done.refs_1_, ...), custom_call_target="tpu_custom_call" | custom-call | tf_op jit(solution)/shard_map/pallas_call | solution.py:417
  130.6 4.6 %all-to-all-start.2 = ((bf16[8,96,640]{2,1,0:T(8,128)(2,1)}), bf16[8,96,640]{2,1,0:T(8,128)(2,1)S(1)}, u32[]{:S(2)}, u32[]{:S(2)}) async-start(bf16[8,96,640]{2,1,0:T(8,128)(2,1)} %get-tuple-element.56), calls=%async_computation.2 | async-start | bytes 1966080 | tf_op jit(solution)/shard_map/all_to_all | solution.py:479
  135.2 3.1 %shard_map.127 = (bf16[768,256]{1,0:T(8,128)(2,1)}, bf16[768,256]{1,0:T(8,128)(2,1)}, bf16[768,256]{1,0:T(8,128)(2,1)}, bf16[384,256]{1,0:T(8,128)(2,1)}, bf16[384,256]{1,0:T(8,128)(2,1)}) custom-call(bf16[4,768,256]{2,1,0:T(8,128)(2,1)} %get-tuple-element.43.keep_ref, bf16[4,768,256]{2,1,0:T(8,128)(2,1)} %collective-permute-done.21.got_ref), custom_call_target="tpu_custom_call" | custom-call | tf_op jit(solution)/shard_map/pallas_call | solution.py:439
  138.3 2.0 collective-permute-start.22
  140.4 1.2 collective-permute-start.23
  141.6 1.2 copy-done.6
  142.8 3.3 %shard_map.125 = (bf16[768,256]{1,0:T(8,128)(2,1)}, bf16[768,256]{1,0:T(8,128)(2,1)}, bf16[768,256]{1,0:T(8,128)(2,1)}, bf16[384,256]{1,0:T(8,128)(2,1)}, bf16[384,256]{1,0:T(8,128)(2,1)}) custom-call(bf16[4,768,256]{2,1,0:T(8,128)(2,1)} %get-tuple-element.34.keep_ref, bf16[4,768,256]{2,1,0:T(8,128)(2,1)} %copy-done.6), custom_call_target="tpu_custom_call" | custom-call | tf_op jit(solution)/shard_map/pallas_call | solution.py:439
  146.0 0.8 collective-permute-start.17
  146.9 2.4 %collective-permute-start.18 = (bf16[384,256]{1,0:T(8,128)(2,1)}, bf16[384,256]{1,0:T(8,128)(2,1)S(1)}, u32[]{:S(2)}, u32[]{:S(2)}) collective-permute-start(bf16[384,256]{1,0:T(8,128)(2,1)} %get-tuple-element.40), channel_id=1, source_target_pairs={{0,192},{64,0},{128,64},{192,128},{1,193},{65,1},{129,65},{193,129... | collective-permute-start | bytes 589832 | tf_op jit(solution)/shard_map/ppermute | solution.py:37
  149.3 5.4 %collective-permute-done.22.up_ref = bf16[384,256]{1,0:T(8,128)(2,1)S(1)} collective-permute-done((bf16[384,256]{1,0:T(8,128)(2,1)}, bf16[384,256]{1,0:T(8,128)(2,1)S(1)}, u32[]{:S(2)}, u32[]{:S(2)}) %collective-permute-start.22) | collective-permute-done | bytes 196640 | tf_op jit(solution)/shard_map/ppermute | solution.py:37
  154.7 0.7 copy-done.19
  155.5 2.2 shard_map.128
  158.0 2.9 %collective-permute-start.25 = (bf16[768,256]{1,0:T(8,128)(2,1)}, bf16[768,256]{1,0:T(8,128)(2,1)S(1)}, u32[]{:S(2)}, u32[]{:S(2)}) collective-permute-start(bf16[768,256]{1,0:T(8,128)(2,1)} %get-tuple-element.51), channel_id=1, source_target_pairs={{0,192},{64,0},{128,64},{192,128},{1,193},{65,1},{129,65},{193,129... | collective-permute-start | bytes 1179656 | tf_op jit(solution)/shard_map/ppermute | solution.py:37
  160.9 0.7 copy-done.18
  161.6 2.2 shard_map.126
  163.8 3.2 %collective-permute-start.20 = (bf16[768,256]{1,0:T(8,128)(2,1)}, bf16[768,256]{1,0:T(8,128)(2,1)S(1)}, u32[]{:S(2)}, u32[]{:S(2)}) collective-permute-start(bf16[768,256]{1,0:T(8,128)(2,1)} %get-tuple-element.42), channel_id=1, source_target_pairs={{0,192},{64,0},{128,64},{192,128},{1,193},{65,1},{129,65},{193,129... | collective-permute-start | bytes 1179656 | tf_op jit(solution)/shard_map/ppermute | solution.py:37
  167.0 4.1 %collective-permute-done.24.refs_5_ = bf16[768,256]{1,0:T(8,128)(2,1)S(1)} collective-permute-done((bf16[768,256]{1,0:T(8,128)(2,1)}, bf16[768,256]{1,0:T(8,128)(2,1)S(1)}, u32[]{:S(2)}, u32[]{:S(2)}) %collective-permute-start.24) | collective-permute-done | bytes 393248 | tf_op jit(solution)/shard_map/ppermute | solution.py:37
  171.1 6.8 %collective-permute-done.19.refs_2_ = bf16[768,256]{1,0:T(8,128)(2,1)S(1)} collective-permute-done((bf16[768,256]{1,0:T(8,128)(2,1)}, bf16[768,256]{1,0:T(8,128)(2,1)S(1)}, u32[]{:S(2)}, u32[]{:S(2)}) %collective-permute-start.19) | collective-permute-done | bytes 393248 | tf_op jit(solution)/shard_map/ppermute | solution.py:37
  178.0 0.7 copy-done.13
  178.9 3.0 %shard_map.129 = (bf16[1280,256]{1,0:T(8,128)(2,1)}, f32[2,128,256]{2,1,0:T(8,128)}) custom-call(bf16[160,160]{1,0:T(8,128)(2,1)} %constant.88.clone.order_ref.refs_0_, bf16[768,256]{1,0:T(8,128)(2,1)} %get-tuple-element.36.refs_1_, bf16[768,256]{1,0:T(8,128)(2,1)} %copy-done.13, bf16[768,256]{1,0:T(8,128)(2,1)} %copy-done.14, ...), custom_call_target="tpu_custom_call" | custom-call | tf_op jit(solution)/shard_map/pallas_call | solution.py:439
  181.9 12.2 %all-to-all-start.1 = ((bf16[32,40,256]{2,1,0:T(8,128)(2,1)}), bf16[32,40,256]{2,1,0:T(8,128)(2,1)S(1)}, u32[]{:S(2)}, u32[]{:S(2)}) async-start(bf16[32,40,256]{2,1,0:T(8,128)(2,1)} %bitcast.27), calls=%async_computation.1 | async-start | bytes 1310720 | tf_op jit(solution)/shard_map/all_to_all | solution.py:468
  194.3 0.8 copy.40.code_ref
  195.1 6.5 %shard_map.131 = bf16[3,176,2048]{2,1,0:T(8,128)(2,1)} custom-call(s32[176,1]{1,0:T(8,128)} %copy.40.code_ref, bf16[8,96,640]{2,1,0:T(8,128)(2,1)} %copy-done, bf16[8,1280,256]{2,1,0:T(8,128)(2,1)} %bitcast.20), custom_call_target="tpu_custom_call" | custom-call | tf_op jit(solution)/shard_map/pallas_call | solution.py:480
  201.6 8.8 %all-to-all-done.1 = bf16[32,40,256]{2,1,0:T(8,128)(2,1)S(1)} async-done(((bf16[32,40,256]{2,1,0:T(8,128)(2,1)}), bf16[32,40,256]{2,1,0:T(8,128)(2,1)S(1)}, u32[]{:S(2)}, u32[]{:S(2)}) %all-to-all-start.1) | async-done | bytes 655392 | tf_op jit(solution)/shard_map/all_to_all | solution.py:468
  210.4 0.8 copy-done.2
  211.3 3.0 %shard_map.130 = (bf16[128,256]{1,0:T(8,128)(2,1)}, bf16[128,256]{1,0:T(8,128)(2,1)}) custom-call(s32[128,4]{1,0:T(8,128)} %copy.38.routes_ref, f32[128,4]{1,0:T(8,128)} %copy.39.gates_ref, s32[8,1280]{1,0:T(8,128)} %constant.87.clone.table_ref, bf16[1280,256]{1,0:T(8,128)(2,1)} %bitcast.23, f32[2,128,256]{2,1,0:T(8,128)} %get-tuple-element.53.own_ref), custom_call_target="tpu_custom_call" | custom-call | tf_op jit(solution)/shard_map/pallas_call | solution.py:471
  (101 shorter events, 6.4 us)
Async XLA Ops:
  7.2 2.1 copy-start.24
  7.2 2.9 %copy-start.25 = (f32[128,4]{0,1:T(4,128)S(1)}, f32[128,4]{0,1:T(4,128)}, u32[]{:S(2)}) copy-start(f32[128,4]{0,1:T(4,128)} %param.14) | copy-start | bytes 6148
  7.2 50.1 %all-gather.4.cloned.1.call-start = ((), (), s32[]{:S(2)}) async-start(), calls=%async_computation.3 | async-start | bytes 1179648 | tf_op jit(solution)/shard_map/all_gather | solution.py:363
  15.2 35.4 %all-to-all-start = ((bf16[32,40,256]{2,1,0:T(8,128)(2,1)}), bf16[32,40,256]{2,1,0:T(8,128)(2,1)S(1)}, u32[]{:S(2)}, u32[]{:S(2)}) async-start(bf16[32,40,256]{2,1,0:T(8,128)(2,1)} %bitcast.22), calls=%async_computation | async-start | bytes 1310720 | tf_op jit(solution)/shard_map/all_to_all | solution.py:388
  26.9 77.2 %all-gather.6.cloned.1.call-start = ((), (), s32[]{:S(2)}) async-start(), calls=%async_computation.4 | async-start | bytes 5898240 | tf_op jit(solution)/shard_map/all_gather | solution.py:415
  27.0 12.6 %copy-start.10 = (bf16[544,128]{1,0:T(8,128)(2,1)}, bf16[544,128]{1,0:T(8,128)(2,1)S(1)}, u32[]{:S(2)}) copy-start(bf16[544,128]{1,0:T(8,128)(2,1)S(1)} %slice.53.refs_0_) | copy-start | bytes 417796
  27.0 6.2 %collective-permute-start.2 = (bf16[544,128]{1,0:T(8,128)(2,1)S(1)}, bf16[544,128]{1,0:T(8,128)(2,1)S(1)}, u32[]{:S(2)}, u32[]{:S(2)}) collective-permute-start(bf16[544,128]{1,0:T(8,128)(2,1)S(1)} %slice.53.refs_0_), channel_id=1, source_target_pairs={{0,8},{8,16},{16,24},{24,0},{1,9},{9,17},{17,25},{25,1},{2,10},{10... | collective-permute-start | bytes 417800 | tf_op jit(solution)/shard_map/ppermute | solution.py:37
  28.6 6.3 %collective-permute-start.3 = (bf16[544,128]{1,0:T(8,128)(2,1)S(1)}, bf16[544,128]{1,0:T(8,128)(2,1)S(1)}, u32[]{:S(2)}, u32[]{:S(2)}) collective-permute-start(bf16[544,128]{1,0:T(8,128)(2,1)S(1)} %slice.53.refs_0_), channel_id=1, source_target_pairs={{0,24},{8,0},{16,8},{24,16},{1,25},{9,1},{17,9},{25,17},{2,26},{10... | collective-permute-start | bytes 417800 | tf_op jit(solution)/shard_map/ppermute | solution.py:37
  33.2 6.4 %copy-start.15 = (bf16[544,128]{1,0:T(8,128)(2,1)}, bf16[544,128]{1,0:T(8,128)(2,1)S(1)}, u32[]{:S(2)}) copy-start(bf16[544,128]{1,0:T(8,128)(2,1)S(1)} %collective-permute-done.2.refs_1_) | copy-start | bytes 417796
  33.2 4.7 %collective-permute-start.4 = (bf16[272,128]{1,0:T(8,128)(2,1)S(1)}, bf16[272,128]{1,0:T(8,128)(2,1)S(1)}, u32[]{:S(2)}, u32[]{:S(2)}) collective-permute-start(bf16[272,128]{1,0:T(8,128)(2,1)S(1)} %slice.54), channel_id=1, source_target_pairs={{0,8},{8,16},{16,24},{24,0},{1,9},{9,17},{17,25},{25,1},{2,10},{10... | collective-permute-start | bytes 208904 | tf_op jit(solution)/shard_map/ppermute | solution.py:37
  34.9 4.7 %copy-start.16 = (bf16[544,128]{1,0:T(8,128)(2,1)}, bf16[544,128]{1,0:T(8,128)(2,1)S(1)}, u32[]{:S(2)}) copy-start(bf16[544,128]{1,0:T(8,128)(2,1)S(1)} %collective-permute-done.3.refs_2_) | copy-start | bytes 417796
  34.9 36.7 %copy-start.26 = (s32[32]{0:T(128)S(1)}, s32[32]{0:T(128)}, u32[]{:S(2)}) copy-start(s32[32]{0:T(128)} %param.16) | copy-start | bytes 388
  34.9 4.7 %collective-permute-start.5 = (bf16[272,128]{1,0:T(8,128)(2,1)S(1)}, bf16[272,128]{1,0:T(8,128)(2,1)S(1)}, u32[]{:S(2)}, u32[]{:S(2)}) collective-permute-start(bf16[272,128]{1,0:T(8,128)(2,1)S(1)} %slice.55), channel_id=1, source_target_pairs={{0,24},{8,0},{16,8},{24,16},{1,25},{9,1},{17,9},{25,17},{2,26},{10... | collective-permute-start | bytes 208904 | tf_op jit(solution)/shard_map/ppermute | solution.py:37
  37.9 1.7 copy-start.22
  39.6 0.6 copy-start.23
  42.2 11.6 %copy-start.5 = (bf16[2176,128]{1,0:T(8,128)(2,1)S(1)}, bf16[2176,128]{1,0:T(8,128)(2,1)}, u32[]{:S(2)}) copy-start(bf16[2176,128]{1,0:T(8,128)(2,1)} %shard_map.122.refs_6_) | copy-start | bytes 1671172
  50.6 0.8 copy-start.1
  53.8 14.6 %collective-permute-start.6 = (bf16[2176,128]{1,0:T(8,128)(2,1)S(1)}, bf16[2176,128]{1,0:T(8,128)(2,1)S(1)}, u32[]{:S(2)}, u32[]{:S(2)}) collective-permute-start(bf16[2176,128]{1,0:T(8,128)(2,1)S(1)} %copy-done.5), channel_id=1, source_target_pairs={{0,1},{1,2},{2,3},{3,4},{4,5},{5,6},{6,7},{7,0},{8,9},{9,10},{10,1... | collective-permute-start | bytes 1671176 | tf_op jit(solution)/shard_map/ppermute | solution.py:37
  56.0 13.7 %collective-permute-start.8 = (bf16[2176,128]{1,0:T(8,128)(2,1)S(1)}, bf16[2176,128]{1,0:T(8,128)(2,1)}, u32[]{:S(2)}, u32[]{:S(2)}) collective-permute-start(bf16[2176,128]{1,0:T(8,128)(2,1)S(1)} %copy-done.5), channel_id=1, source_target_pairs={{0,7},{1,0},{2,1},{3,2},{4,3},{5,4},{6,5},{7,6},{8,15},{9,8},{10,9... | collective-permute-start | bytes 1671176 | tf_op jit(solution)/shard_map/ppermute | solution.py:37
  57.3 28.5 %collective-permute-start = (bf16[4096,128]{1,0:T(8,128)(2,1)}, bf16[4096,128]{1,0:T(8,128)(2,1)S(1)}, u32[]{:S(2)}, u32[]{:S(2)}) collective-permute-start(bf16[4096,128]{1,0:T(8,128)(2,1)} %all-gather.4.cloned.1.call-done.refs_1_), channel_id=1, source_target_pairs={{0,8},{8,16},{16,24},{24,0},{1,9},{9,17},{17,25},{25,1},{2,10},{10... | collective-permute-start | bytes 3145736 | tf_op jit(solution)/shard_map/ppermute | solution.py:37
  58.4 27.3 %collective-permute-start.1 = (bf16[4096,128]{1,0:T(8,128)(2,1)}, bf16[4096,128]{1,0:T(8,128)(2,1)S(1)}, u32[]{:S(2)}, u32[]{:S(2)}) collective-permute-start(bf16[4096,128]{1,0:T(8,128)(2,1)} %all-gather.4.cloned.1.call-done.refs_1_), channel_id=1, source_target_pairs={{0,24},{8,0},{16,8},{24,16},{1,25},{9,1},{17,9},{25,17},{2,26},{10... | collective-permute-start | bytes 3145736 | tf_op jit(solution)/shard_map/ppermute | solution.py:37
  68.4 14.2 %copy-start.9 = (bf16[2176,128]{1,0:T(8,128)(2,1)}, bf16[2176,128]{1,0:T(8,128)(2,1)S(1)}, u32[]{:S(2)}) copy-start(bf16[2176,128]{1,0:T(8,128)(2,1)S(1)} %collective-permute-done.6.refs_7_) | copy-start | bytes 1671172
  68.4 13.7 %collective-permute-start.7 = (bf16[2176,128]{1,0:T(8,128)(2,1)S(1)}, bf16[2176,128]{1,0:T(8,128)(2,1)}, u32[]{:S(2)}, u32[]{:S(2)}) collective-permute-start(bf16[2176,128]{1,0:T(8,128)(2,1)S(1)} %collective-permute-done.6.refs_7_), channel_id=1, source_target_pairs={{0,1},{1,2},{2,3},{3,4},{4,5},{5,6},{6,7},{7,0},{8,9},{9,10},{10,1... | collective-permute-start | bytes 1671176 | tf_op jit(solution)/shard_map/ppermute | solution.py:37
  69.6 13.0 %collective-permute-start.9 = (bf16[2176,128]{1,0:T(8,128)(2,1)}, bf16[2176,128]{1,0:T(8,128)(2,1)}, u32[]{:S(2)}, u32[]{:S(2)}) collective-permute-start(bf16[2176,128]{1,0:T(8,128)(2,1)} %collective-permute-done.8.refs_8_), channel_id=1, source_target_pairs={{0,7},{1,0},{2,1},{3,2},{4,3},{5,4},{6,5},{7,6},{8,15},{9,8},{10,9... | collective-permute-start | bytes 1671176 | tf_op jit(solution)/shard_map/ppermute | solution.py:37
  82.1 12.9 %collective-permute-start.12 = (bf16[2176,128]{1,0:T(8,128)(2,1)}, bf16[2176,128]{1,0:T(8,128)(2,1)S(1)}, u32[]{:S(2)}, u32[]{:S(2)}) collective-permute-start(bf16[2176,128]{1,0:T(8,128)(2,1)} %collective-permute-done.7.refs_9_), channel_id=1, source_target_pairs={{0,1},{1,2},{2,3},{3,4},{4,5},{5,6},{6,7},{7,0},{8,9},{9,10},{10,1... | collective-permute-start | bytes 1671176 | tf_op jit(solution)/shard_map/ppermute | solution.py:37
  82.6 13.2 %collective-permute-start.13 = (bf16[2176,128]{1,0:T(8,128)(2,1)}, bf16[2176,128]{1,0:T(8,128)(2,1)S(1)}, u32[]{:S(2)}, u32[]{:S(2)}) collective-permute-start(bf16[2176,128]{1,0:T(8,128)(2,1)} %collective-permute-done.9.refs_10_), channel_id=1, source_target_pairs={{0,7},{1,0},{2,1},{3,2},{4,3},{5,4},{6,5},{7,6},{8,15},{9,8},{10,9... | collective-permute-start | bytes 1671176 | tf_op jit(solution)/shard_map/ppermute | solution.py:37
  85.8 10.8 %copy-start.3 = (bf16[4096,128]{1,0:T(8,128)(2,1)}, bf16[4096,128]{1,0:T(8,128)(2,1)S(1)}, u32[]{:S(2)}) copy-start(bf16[4096,128]{1,0:T(8,128)(2,1)S(1)} %collective-permute-done.refs_2_) | copy-start | bytes 3145732
  85.8 10.8 %copy-start.4 = (bf16[4096,128]{1,0:T(8,128)(2,1)}, bf16[4096,128]{1,0:T(8,128)(2,1)S(1)}, u32[]{:S(2)}) copy-start(bf16[4096,128]{1,0:T(8,128)(2,1)S(1)} %collective-permute-done.1.refs_3_) | copy-start | bytes 3145732
  86.7 17.5 %collective-permute-start.10 = (bf16[2048,128]{1,0:T(8,128)(2,1)}, bf16[2048,128]{1,0:T(8,128)(2,1)}, u32[]{:S(2)}, u32[]{:S(2)}) collective-permute-start(bf16[2048,128]{1,0:T(8,128)(2,1)} %slice.45), channel_id=1, source_target_pairs={{0,8},{8,16},{16,24},{24,0},{1,9},{9,17},{17,25},{25,1},{2,10},{10... | collective-permute-start | bytes 1572872 | tf_op jit(solution)/shard_map/ppermute | solution.py:37
  89.0 15.2 %collective-permute-start.11 = (bf16[2048,128]{1,0:T(8,128)(2,1)}, bf16[2048,128]{1,0:T(8,128)(2,1)}, u32[]{:S(2)}, u32[]{:S(2)}) collective-permute-start(bf16[2048,128]{1,0:T(8,128)(2,1)} %slice.46), channel_id=1, source_target_pairs={{0,24},{8,0},{16,8},{24,16},{1,25},{9,1},{17,9},{25,17},{2,26},{10... | collective-permute-start | bytes 1572872 | tf_op jit(solution)/shard_map/ppermute | solution.py:37
  95.0 9.2 %copy-start.7 = (bf16[2176,128]{1,0:T(8,128)(2,1)}, bf16[2176,128]{1,0:T(8,128)(2,1)S(1)}, u32[]{:S(2)}) copy-start(bf16[2176,128]{1,0:T(8,128)(2,1)S(1)} %collective-permute-done.12.refs_11_) | copy-start | bytes 1671172
  95.8 8.0 %collective-permute-start.14 = (bf16[1088,128]{1,0:T(8,128)(2,1)}, bf16[1088,128]{1,0:T(8,128)(2,1)S(1)}, u32[]{:S(2)}, u32[]{:S(2)}) collective-permute-start(bf16[1088,128]{1,0:T(8,128)(2,1)} %slice.56), channel_id=1, source_target_pairs={{0,1},{1,2},{2,3},{3,4},{4,5},{5,6},{6,7},{7,0},{8,9},{9,10},{10,1... | collective-permute-start | bytes 835592 | tf_op jit(solution)/shard_map/ppermute | solution.py:37
  95.8 8.4 %copy-start.8 = (bf16[2176,128]{1,0:T(8,128)(2,1)}, bf16[2176,128]{1,0:T(8,128)(2,1)S(1)}, u32[]{:S(2)}) copy-start(bf16[2176,128]{1,0:T(8,128)(2,1)S(1)} %collective-permute-done.13.refs_12_) | copy-start | bytes 1671172
  96.5 7.6 %collective-permute-start.15 = (bf16[1088,128]{1,0:T(8,128)(2,1)}, bf16[1088,128]{1,0:T(8,128)(2,1)}, u32[]{:S(2)}, u32[]{:S(2)}) collective-permute-start(bf16[1088,128]{1,0:T(8,128)(2,1)} %slice.57), channel_id=1, source_target_pairs={{0,7},{1,0},{2,1},{3,2},{4,3},{5,4},{6,5},{7,6},{8,15},{9,8},{10,9... | collective-permute-start | bytes 835592 | tf_op jit(solution)/shard_map/ppermute | solution.py:37
  103.7 0.7 copy-start.17
  130.0 5.2 %collective-permute-start.21 = (bf16[4,768,256]{2,1,0:T(8,128)(2,1)}, bf16[4,768,256]{2,1,0:T(8,128)(2,1)}, u32[]{:S(2)}, u32[]{:S(2)}) collective-permute-start(bf16[4,768,256]{2,1,0:T(8,128)(2,1)} %get-tuple-element.44), channel_id=1, source_target_pairs={{0,32},{32,0},{1,33},{33,1},{2,34},{34,2},{3,35},{35,3},{4,36},{36... | collective-permute-start | bytes 4718600 | tf_op jit(solution)/shard_map/ppermute | solution.py:37
  130.1 11.5 %collective-permute-start.16 = (bf16[4,768,256]{2,1,0:T(8,128)(2,1)}, bf16[4,768,256]{2,1,0:T(8,128)(2,1)S(1)}, u32[]{:S(2)}, u32[]{:S(2)}) collective-permute-start(bf16[4,768,256]{2,1,0:T(8,128)(2,1)} %get-tuple-element.35), channel_id=1, source_target_pairs={{0,32},{32,0},{1,33},{33,1},{2,34},{34,2},{3,35},{35,3},{4,36},{36... | collective-permute-start | bytes 4718600 | tf_op jit(solution)/shard_map/ppermute | solution.py:37
  130.6 51.3 %all-to-all-start.2 = ((bf16[8,96,640]{2,1,0:T(8,128)(2,1)}), bf16[8,96,640]{2,1,0:T(8,128)(2,1)S(1)}, u32[]{:S(2)}, u32[]{:S(2)}) async-start(bf16[8,96,640]{2,1,0:T(8,128)(2,1)} %get-tuple-element.56), calls=%async_computation.2 | async-start | bytes 1966080 | tf_op jit(solution)/shard_map/all_to_all | solution.py:479
  138.3 16.4 %collective-permute-start.22 = (bf16[384,256]{1,0:T(8,128)(2,1)}, bf16[384,256]{1,0:T(8,128)(2,1)S(1)}, u32[]{:S(2)}, u32[]{:S(2)}) collective-permute-start(bf16[384,256]{1,0:T(8,128)(2,1)} %get-tuple-element.48), channel_id=1, source_target_pairs={{0,64},{64,128},{128,192},{192,0},{1,65},{65,129},{129,193},{193,1... | collective-permute-start | bytes 589832 | tf_op jit(solution)/shard_map/ppermute | solution.py:37
  140.4 14.4 %collective-permute-start.23 = (bf16[384,256]{1,0:T(8,128)(2,1)}, bf16[384,256]{1,0:T(8,128)(2,1)S(1)}, u32[]{:S(2)}, u32[]{:S(2)}) collective-permute-start(bf16[384,256]{1,0:T(8,128)(2,1)} %get-tuple-element.49), channel_id=1, source_target_pairs={{0,192},{64,0},{128,64},{192,128},{1,193},{65,1},{129,65},{193,129... | collective-permute-start | bytes 589832 | tf_op jit(solution)/shard_map/ppermute | solution.py:37
  141.6 1.2 copy-start.6
  146.0 14.8 %collective-permute-start.17 = (bf16[384,256]{1,0:T(8,128)(2,1)}, bf16[384,256]{1,0:T(8,128)(2,1)S(1)}, u32[]{:S(2)}, u32[]{:S(2)}) collective-permute-start(bf16[384,256]{1,0:T(8,128)(2,1)} %get-tuple-element.39), channel_id=1, source_target_pairs={{0,64},{64,128},{128,192},{192,0},{1,65},{65,129},{129,193},{193,1... | collective-permute-start | bytes 589832 | tf_op jit(solution)/shard_map/ppermute | solution.py:37
  146.9 14.0 %collective-permute-start.18 = (bf16[384,256]{1,0:T(8,128)(2,1)}, bf16[384,256]{1,0:T(8,128)(2,1)S(1)}, u32[]{:S(2)}, u32[]{:S(2)}) collective-permute-start(bf16[384,256]{1,0:T(8,128)(2,1)} %get-tuple-element.40), channel_id=1, source_target_pairs={{0,192},{64,0},{128,64},{192,128},{1,193},{65,1},{129,65},{193,129... | collective-permute-start | bytes 589832 | tf_op jit(solution)/shard_map/ppermute | solution.py:37
  154.7 0.7 copy-start.19
  154.7 0.7 copy-start.21
  157.6 13.5 %collective-permute-start.24 = (bf16[768,256]{1,0:T(8,128)(2,1)}, bf16[768,256]{1,0:T(8,128)(2,1)S(1)}, u32[]{:S(2)}, u32[]{:S(2)}) collective-permute-start(bf16[768,256]{1,0:T(8,128)(2,1)} %get-tuple-element.50), channel_id=1, source_target_pairs={{0,64},{64,128},{128,192},{192,0},{1,65},{65,129},{129,193},{193,1... | collective-permute-start | bytes 1179656 | tf_op jit(solution)/shard_map/ppermute | solution.py:37
  158.0 13.1 %collective-permute-start.25 = (bf16[768,256]{1,0:T(8,128)(2,1)}, bf16[768,256]{1,0:T(8,128)(2,1)S(1)}, u32[]{:S(2)}, u32[]{:S(2)}) collective-permute-start(bf16[768,256]{1,0:T(8,128)(2,1)} %get-tuple-element.51), channel_id=1, source_target_pairs={{0,192},{64,0},{128,64},{192,128},{1,193},{65,1},{129,65},{193,129... | collective-permute-start | bytes 1179656 | tf_op jit(solution)/shard_map/ppermute | solution.py:37
  160.9 0.7 copy-start.18
  160.9 0.7 copy-start.20
  163.8 14.2 %collective-permute-start.19 = (bf16[768,256]{1,0:T(8,128)(2,1)}, bf16[768,256]{1,0:T(8,128)(2,1)S(1)}, u32[]{:S(2)}, u32[]{:S(2)}) collective-permute-start(bf16[768,256]{1,0:T(8,128)(2,1)} %get-tuple-element.41), channel_id=1, source_target_pairs={{0,64},{64,128},{128,192},{192,0},{1,65},{65,129},{129,193},{193,1... | collective-permute-start | bytes 1179656 | tf_op jit(solution)/shard_map/ppermute | solution.py:37
  163.8 14.2 %collective-permute-start.20 = (bf16[768,256]{1,0:T(8,128)(2,1)}, bf16[768,256]{1,0:T(8,128)(2,1)S(1)}, u32[]{:S(2)}, u32[]{:S(2)}) collective-permute-start(bf16[768,256]{1,0:T(8,128)(2,1)} %get-tuple-element.42), channel_id=1, source_target_pairs={{0,192},{64,0},{128,64},{192,128},{1,193},{65,1},{129,65},{193,129... | collective-permute-start | bytes 1179656 | tf_op jit(solution)/shard_map/ppermute | solution.py:37
  171.1 6.9 %copy-start.11 = (bf16[768,256]{1,0:T(8,128)(2,1)}, bf16[768,256]{1,0:T(8,128)(2,1)S(1)}, u32[]{:S(2)}) copy-start(bf16[768,256]{1,0:T(8,128)(2,1)S(1)} %collective-permute-done.24.refs_5_) | copy-start | bytes 1179652
  171.1 6.9 %copy-start.12 = (bf16[768,256]{1,0:T(8,128)(2,1)}, bf16[768,256]{1,0:T(8,128)(2,1)S(1)}, u32[]{:S(2)}) copy-start(bf16[768,256]{1,0:T(8,128)(2,1)S(1)} %collective-permute-done.25.refs_6_) | copy-start | bytes 1179652
  178.0 0.7 copy-start.13
  178.0 0.9 copy-start.14
  181.9 13.2 %copy-start = (bf16[8,96,640]{2,1,0:T(8,128)(2,1)}, bf16[8,96,640]{2,1,0:T(8,128)(2,1)S(1)}, u32[]{:S(2)}) copy-start(bf16[8,96,640]{2,1,0:T(8,128)(2,1)S(1)} %all-to-all-done.2.acts_ref) | copy-start | bytes 2949124
  181.9 28.5 %all-to-all-start.1 = ((bf16[32,40,256]{2,1,0:T(8,128)(2,1)}), bf16[32,40,256]{2,1,0:T(8,128)(2,1)S(1)}, u32[]{:S(2)}, u32[]{:S(2)}) async-start(bf16[32,40,256]{2,1,0:T(8,128)(2,1)} %bitcast.27), calls=%async_computation.1 | async-start | bytes 1310720 | tf_op jit(solution)/shard_map/all_to_all | solution.py:468
  210.4 0.8 copy-start.2
Sparse Core Ops, SparseCore 0:
  9.8 47.4 all-gather.3
  59.1 38.4 all-gather.5
